TPU v7x, 512 devices: a whole 4x4x16 slice. The times are simulated.
512 devices in a mesh: dp: 32 (over x_lo, z), blk: 16 (over y, x_hi, core).
Axes of the slice: x: 4 (x_hi: 2, x_lo: 2; x = x_hi * 2 + x_lo), y: 4, z: 16, core: 2. Of those that a mesh axis runs over, the one named last changes fastest.
Arguments:
- tokens: bfloat16 [131072, 1024], P(('dp', 'blk')), may hold values from -6 to 6
- lengths: int32 [4096], P(('dp', 'blk')), may hold values from 1 to 32
- cotangent: bfloat16 [131072, 1024], P(('dp', 'blk')), may hold values from -6 to 6
- input_weight: bfloat16 [1024, 1536], P('blk'), may hold values from -0.1875 to 0.1875
- output_weight: bfloat16 [1024, 512], P('blk'), may hold values from -0.25 to 0.25
Outputs:
- layer_out: bfloat16 [131072, 1024], P(('dp', 'blk'))
- grad_tokens: bfloat16 [131072, 1024], P(('dp', 'blk'))
- grad_input_weight: float32 [1024, 1536], P('blk')
- grad_output_weight: float32 [1024, 512], P('blk')
Inputs may be any that keep to these rules, and one draw needn't show every extreme that they name: `lengths`: number of real tokens of each caption; tokens past it are padding.
All inputs are finite; a program needn't handle non-finite values.
Results may differ from a plain program's by a relative error of at most 0.035.
Values may be sent and summed in bfloat16 or wider, within the bound.
A program may use at most 64 MiB of HBM per device.

v0:
```python
import jax
import jax.numpy as jnp
from jax import lax
from jax.sharding import PartitionSpec as P

HEADS = 8
HEAD_SIZE = 64
CAPLEN = 32


EPSILON = 1e-06


def attend_local(projected, lengths, head_dim):
    captions = projected.shape[0] // CAPLEN
    query_rows = projected[:, :head_dim].reshape(captions, CAPLEN, HEADS, HEAD_SIZE)
    key_rows = projected[:, head_dim : 2 * head_dim].reshape(captions, CAPLEN, HEADS, HEAD_SIZE)
    value_rows = projected[:, 2 * head_dim :].reshape(captions, CAPLEN, HEADS, HEAD_SIZE)
    scores = jnp.einsum(
        "clhe,cmhe->chlm", query_rows, key_rows, preferred_element_type=jnp.float32
    ) * HEAD_SIZE ** (-0.5)
    position = jnp.arange(CAPLEN, dtype=jnp.int32)
    causal = position[None, :] <= position[:, None]
    allowed = causal[None, :, :] & (position[None, None, :] < lengths[:, None, None])
    raised = jnp.where(allowed[:, None, :, :], jnp.exp(scores), jnp.float32(0.0))
    probability = raised / jnp.sum(raised, axis=-1, keepdims=True)
    rounded_prob = probability.astype(jnp.bfloat16)
    attended = jnp.einsum(
        "chlm,cmhe->clhe", rounded_prob, value_rows, preferred_element_type=jnp.float32
    )
    attended = attended.reshape(projected.shape[0], head_dim).astype(jnp.bfloat16)
    return (attended, probability, rounded_prob, query_rows, key_rows, value_rows)


def per_device(tokens, lengths, cotangent, input_weight, output_weight):
    head_dim = output_weight.shape[1]
    row_count = tokens.shape[0]
    captions = row_count // CAPLEN
    score_scale = HEAD_SIZE ** (-0.5)
    floats = tokens.astype(jnp.float32)
    inverse = lax.rsqrt(jnp.mean(floats * floats, axis=-1, keepdims=True) + EPSILON)
    normed = (floats * inverse).astype(jnp.bfloat16)
    contract_last = (((1,), (1,)), ((), ()))
    contract_first = (((0,), (0,)), ((), ()))
    columns = normed
    projected = jnp.dot(
        columns,
        lax.all_gather(input_weight, "blk", axis=0, tiled=True),
        preferred_element_type=jnp.float32,
    ).astype(jnp.bfloat16)
    attended, probability, rounded_prob, query_rows, key_rows, value_rows = attend_local(
        projected, lengths, head_dim
    )
    mixed = lax.dot_general(
        attended,
        lax.all_gather(output_weight, "blk", axis=0, tiled=True),
        contract_last,
        preferred_element_type=jnp.float32,
    )
    layer_out = (floats + mixed).astype(jnp.bfloat16)
    columns = cotangent
    grad_attended = jnp.dot(
        columns,
        lax.all_gather(output_weight, "blk", axis=0, tiled=True),
        preferred_element_type=jnp.float32,
    ).astype(jnp.bfloat16)
    grad_heads = grad_attended.reshape(captions, CAPLEN, HEADS, HEAD_SIZE)
    grad_prob = jnp.einsum(
        "clhe,cmhe->chlm", grad_heads, value_rows, preferred_element_type=jnp.float32
    )
    grad_values = jnp.einsum(
        "chlm,clhe->cmhe", rounded_prob, grad_heads, preferred_element_type=jnp.float32
    )
    grad_scores = (
        probability
        * (grad_prob - jnp.sum(probability * grad_prob, axis=-1, keepdims=True))
        * score_scale
    )
    grad_queries = jnp.einsum("chlm,cmhe->clhe", grad_scores, key_rows.astype(jnp.float32))
    grad_keys = jnp.einsum("chlm,clhe->cmhe", grad_scores, query_rows.astype(jnp.float32))
    grad_projected = jnp.concatenate(
        [
            grad_queries.reshape(row_count, head_dim),
            grad_keys.reshape(row_count, head_dim),
            grad_values.reshape(row_count, head_dim),
        ],
        axis=1,
    ).astype(jnp.bfloat16)
    grad_normed = lax.dot_general(
        grad_projected,
        lax.all_gather(input_weight, "blk", axis=0, tiled=True),
        contract_last,
        preferred_element_type=jnp.float32,
    )
    grad_tokens = (
        cotangent.astype(jnp.float32)
        + inverse * grad_normed
        - floats * inverse**3 * jnp.mean(grad_normed * floats, axis=-1, keepdims=True)
    )
    term_project = lax.dot_general(
        normed, grad_projected, contract_first, preferred_element_type=jnp.float32
    )
    term_output = lax.dot_general(
        cotangent, attended, contract_first, preferred_element_type=jnp.float32
    )
    owned = lax.psum_scatter(
        jnp.concatenate([term_project, term_output], axis=1).astype(jnp.bfloat16),
        "blk",
        scatter_dimension=0,
        tiled=True,
    ).astype(jnp.float32)
    grad_input_weight, grad_output_weight = (
        lax.psum(owned[:, : 3 * head_dim].astype(jnp.bfloat16), "dp").astype(jnp.float32),
        lax.psum(owned[:, 3 * head_dim :].astype(jnp.bfloat16), "dp").astype(jnp.float32),
    )
    return (layer_out, grad_tokens.astype(jnp.bfloat16), grad_input_weight, grad_output_weight)


def solution(mesh):
    placed = (
        P(("dp", "blk"), None),
        P(("dp", "blk")),
        P(("dp", "blk"), None),
        P("blk", None),
        P("blk", None),
    )
    return jax.shard_map(
        per_device,
        mesh=mesh,
        in_specs=placed,
        out_specs=(P(("dp", "blk"), None), P(("dp", "blk"), None), P("blk", None), P("blk", None)),
        check_vma=False,
    )
```

profile of v0, /device:TPU:24, one launch (start us, length us, event | category | flops | bytes accessed | tf_op | source)
XLA Modules:
  0.0 540.0 jit_solution(5313731806655475357)
XLA Ops:
  7.2 0.0 copy-start
  7.2 0.0 all-gather.5.cloned.1.call-start
  7.2 0.7 all-gather.5.cloned.1.call-update
  7.9 0.0 all-gather.3.cloned.1.call-start
  8.0 0.7 all-gather.3.cloned.1.call-update
  8.7 0.0 reduce-scatter.2.cloned.1.call-start
  8.7 1.2 fusion.8
  9.9 0.7 iota_compare_fusion.1
  10.7 0.1 broadcast_and_fusion
  10.8 64.6 %all-gather.5.cloned.1.call-done = bf16[1024,512]{1,0:T(8,128)(2,1)} async-done(((bf16[64,512]{1,0:T(8,128)(2,1)}), bf16[1024,512]{1,0:T(8,128)(2,1)}) %all-gather.5.cloned.1.call-update) | async-done | bytes 1048592 | tf_op jit(solution)/shard_map/all_gather | solution.py:56
  75.4 1.8 convolution_convert_fusion.7
  77.2 0.3 reshape.91
  77.5 66.2 %all-gather.3.cloned.1.call-done = bf16[1024,1536]{1,0:T(8,128)(2,1)} async-done(((bf16[64,1536]{1,0:T(8,128)(2,1)}), bf16[1024,1536]{1,0:T(8,128)(2,1)}) %all-gather.3.cloned.1.call-update) | async-done | bytes 3145744 | tf_op jit(solution)/shard_map/all_gather | solution.py:48
  143.7 0.0 copy-done
  143.7 2.9 convolution_convert_fusion.1
  146.6 0.1 fusion.35
  146.7 0.3 reshape.89
  147.0 0.3 reshape.90
  147.3 0.0 copy-start.3
  147.3 0.3 reshape.88
  147.5 1.4 fusion.2
  148.9 0.0 copy-done.3
  148.9 2.7 fusion.7
  151.7 0.4 fusion.17
  152.0 2.8 fusion.6
  154.8 1.9 multiply_reduce_fusion
  156.7 0.0 copy-start.4
  156.7 2.9 fusion.5
  159.6 0.0 copy-done.4
  159.6 0.0 copy-start.7
  159.6 0.0 copy-start.6
  159.6 3.0 fusion.4
  162.5 0.0 copy-done.7
  162.5 0.0 copy-start.5
  162.5 0.2 copy.33
  162.8 0.3 reshape.94
  163.1 0.0 copy-done.6
  163.1 0.0 copy-start.1
  163.1 0.2 copy.24
  163.3 0.3 convert_element_type.52
  163.6 1.3 copy.29
  164.9 0.3 reshape.92
  165.2 0.0 copy-done.5
  165.2 0.2 copy.31
  165.5 0.3 reshape.93
  165.8 0.0 copy-done.1
  165.8 0.5 fusion
  166.4 1.1 convolution_convert_fusion
  167.5 2.6 pad_maximum_fusion
  170.0 0.0 reduce-scatter.2.cloned.1.call-update
  170.1 0.0 copy-start.2
  170.1 0.0 all-reduce.3.cloned.1.call-start
  170.1 3.1 fusion.13
  173.2 1.1 fusion.12
  174.3 98.5 %reduce-scatter.2.cloned.1.call-done = bf16[64,2048]{1,0:T(8,128)(2,1)} async-done(((bf16[1024,2048]{1,0:T(8,128)(2,1)}), bf16[64,2048]{1,0:T(8,128)(2,1)}) %reduce-scatter.2.cloned.1.call-update) | async-done | bytes 262160 | tf_op jit(solution)/shard_map/reduce_scatter | solution.py:106
  272.8 1.5 slice.26
  274.3 1.6 slice.25
  275.9 0.0 all-reduce.3.cloned.1.call-update
  275.9 0.0 copy-done.2
  275.9 1.3 fusion.3
  277.2 253.1 %all-reduce.3.cloned.1.call-done = (bf16[64,1536]{1,0:T(8,128)(2,1)}, bf16[64,512]{1,0:T(8,128)(2,1)}) async-done(((bf16[64,1536]{1,0:T(8,128)(2,1)}, bf16[64,512]{1,0:T(8,128)(2,1)}), (bf16[64,1536]{1,0:T(8,128)(2,1)}, bf16[64,512]{1,0:T(8,128)(2,1)})) %all-reduce.3.cloned.1.call-update) | async-done | bytes 262160 | tf_op jit(solution)/shard_map/psum | solution.py:113
  530.3 1.5 convert_element_type.58
  531.8 1.7 convert_element_type.57
  (6 shorter events, 0.1 us)
Async XLA Ops:
  7.2 136.5 %copy-start = (bf16[256,1024]{1,0:T(8,128)(2,1)S(1)}, bf16[256,1024]{1,0:T(8,128)(2,1)}, u32[]{:S(2)}) copy-start(bf16[256,1024]{1,0:T(8,128)(2,1)} %param.5) | copy-start | bytes 1572868
  7.2 68.2 %all-gather.5.cloned.1.call-start = ((), (), s32[]{:S(2)}) async-start(), calls=%async_computation.2 | async-start | bytes 1114112 | tf_op jit(solution)/shard_map/all_gather | solution.py:56
  7.9 135.8 %all-gather.3.cloned.1.call-start = ((), (), s32[]{:S(2)}) async-start(), calls=%async_computation.1 | async-start | bytes 3342336 | tf_op jit(solution)/shard_map/all_gather | solution.py:48
  8.7 264.1 %reduce-scatter.2.cloned.1.call-start = ((), (), s32[]{:S(2)}) async-start(), calls=%async_computation.3 | async-start | bytes 4456448 | tf_op jit(solution)/shard_map/reduce_scatter | solution.py:106
  147.3 1.7 copy-start.3
  156.7 2.9 copy-start.4
  159.6 3.0 copy-start.7
  159.6 3.5 copy-start.6
  162.5 2.7 copy-start.5
  163.1 2.7 copy-start.1
  170.1 105.9 %copy-start.2 = (bf16[1024,512]{1,0:T(8,128)(2,1)S(1)}, bf16[1024,512]{1,0:T(8,128)(2,1)}, u32[]{:S(2)}) copy-start(bf16[1024,512]{1,0:T(8,128)(2,1)} %all-gather.5.cloned.1.call-done) | copy-start | bytes 3145732
  170.1 360.2 %all-reduce.3.cloned.1.call-start = ((), (), s32[]{:S(2)}) async-start(), calls=%async_computation.4 | async-start | bytes 524288 | tf_op jit(solution)/shard_map/psum | solution.py:113
Sparse Core Ops, SparseCore 0:
  11.3 63.9 all-gather.4
  78.7 64.9 all-gather.2
  170.2 102.5 reduce-scatter.1
  276.5 253.7 all-reduce.2
where the time goes:
time: 541 us; the launch traced here: 540 us
  waiting for transfers between devices  484 us (89%)
  matrix products  23.8 us (4%)
  between operations  14 us (3%)
  other arithmetic  10.9 us (2%)
  local copies, waits for them, and re-layouts  7.5 us (1%)
    psum x1, waiting for transfers between devices, per_device(): lax.psum(owned[:, :3 * head_dim].astype(jnp.bfloat16), 'dp')  253 us
    reduce_scatter x1, waiting for transfers between devices, per_device(): lax.psum_scatter(jnp.concatenate([term_project, term_output], axis=1).ast...  98.5 us
    all_gather x1, waiting for transfers between devices, per_device(): lax.all_gather(input_weight, 'blk', axis=0, tiled=True)  66.2 us
    all_gather x1, waiting for transfers between devices, per_device(): lax.all_gather(output_weight, 'blk', axis=0, tiled=True)  64.6 us
  transfers between devices with their start and end apart: 4, of which 4 were waited for; matrix products, arithmetic and copies ran while one was open for 2% of the time, Pallas kernels for 0%

commit v1 on v0

v1 whole, which is shorter than its diff:
```python
import functools

import jax
import jax.numpy as jnp
from jax import lax
from jax.experimental import pallas as pl
from jax.experimental.pallas import tpu as pltpu
from jax.sharding import PartitionSpec as P

HEADS = 8
HEAD_SIZE = 64
CAPLEN = 32
EPSILON = 1e-06

MESH = pl.DeviceIdType.MESH
NX, NY, NZ = 4, 4, 16
ROWS = 256
D = 1024
HALF = 256
TILE = 128
BF = jnp.bfloat16
F32 = jnp.float32

GATHER = [(cross, dy, dc) for cross in (0, 1) for dy in range(4) for dc in range(2) if cross or dy or dc]
PLANE = [(dx, dy) for dx in range(4) for dy in range(4) if dx or dy]


def device(x, y, z, c):
    return {"dp": (x % 2) * NZ + z, "blk": y * 4 + (x // 2) * 2 + c}


def dot(a, b, ca, cb):
    return lax.dot_general(a, b, (((ca,), (cb,)), ((), ())), preferred_element_type=F32)


def kernel(
    tok_ref, cot_ref, valid_ref, win_ref, wout_ref,
    lo_ref, gt_ref, gin_ref, gout_ref,
    stage, w, tok2, cot2, valid2, normed, normed_t, cot_t, inverse, proj, gatt, att, grads,
    terms, plane_in, acc, z_in, red, zfin, fin, mixed_out, gn_out, mixed_in, gn_in, gn_own,
    g_send, g_recv, s_send, s_recv, p_send, p_recv, z_send, z_recv, a_send, a_recv, f_send, f_recv,
):
    dp, blk = lax.axis_index("dp"), lax.axis_index("blk")
    xl, z = dp // NZ, dp % NZ
    y, xh, c = blk // 4, (blk // 2) % 2, blk % 2
    x = xh * 2 + xl
    sibling = device(x, y, z, 1 - c)

    def gather_to(cross, dy, dc):
        tx = 3 - x if cross else x
        return device(tx, (y + dy) % NY, z, (c + dc) % 2), (c + dc) % 2

    barrier = pltpu.get_barrier_semaphore()
    greet = [gather_to(*o)[0] for o in GATHER]
    greet += [device((x + dx) % NX, (y + dy) % NY, z, c) for dx, dy in PLANE]
    greet += [device(x, y, (z + dz) % NZ, c) for dz in range(1, NZ)]
    greet += [device(xh * 2 + 1 - xl, y, z, t) for t in range(2)]
    for d in greet:
        pl.semaphore_signal(barrier, inc=1, device_id=d, device_id_type=MESH)

    for h in range(2):
        for part in range(3):
            stage[h, :, part * HALF : (part + 1) * HALF] = win_ref[:, part * 2 * HALF + h * HALF : part * 2 * HALF + (h + 1) * HALF]
        stage[h, :, 3 * HALF :] = wout_ref[:, h * HALF : (h + 1) * HALF]
    my_rows = pl.ds(pl.multiple_of(blk * 64, 64), 64)

    def copy(src, dst, ss, rs, to):
        return pltpu.make_async_remote_copy(src_ref=src, dst_ref=dst, send_sem=ss, recv_sem=rs, device_id=to, device_id_type=MESH)

    def normalise(src, at):
        @pl.loop(0, 2)
        def _(i):
            rows = pl.ds(pl.multiple_of(i * 128, 128), 128)
            out = pl.ds(pl.multiple_of(at + i * 128, 128), 128)
            floats = src[rows, :].astype(F32)
            inv = lax.rsqrt(jnp.mean(floats * floats, axis=-1, keepdims=True) + EPSILON)
            inverse[out, :] = jnp.broadcast_to(inv, (128, 128))
            normed[out, :] = (floats * inv).astype(BF)

    pl.semaphore_wait(barrier, len(greet))

    gathers = []
    for j, o in enumerate(GATHER):
        to, h = gather_to(*o)
        cp = copy(stage.at[h], w.at[my_rows], g_send.at[j], g_recv.at[j], to)
        cp.start()
        gathers.append(cp)
    shares = [
        copy(tok_ref, tok2, s_send.at[0], s_recv.at[0], sibling),
        copy(cot_ref, cot2, s_send.at[1], s_recv.at[1], sibling),
        copy(valid_ref, valid2, s_send.at[2], s_recv.at[2], sibling),
    ]
    for cp in shares:
        cp.start()
    w[my_rows, :] = stage[c]

    normalise(tok_ref, 0)
    for cp in shares:
        cp.wait()
    normalise(tok2, ROWS)

    @pl.loop(0, 4)
    def _(i):
        cols = pl.ds(pl.multiple_of(i * 256, 256), 256)
        normed_t[cols, :] = normed[:, cols].T
        cot_t[cols, 0:ROWS] = cot_ref[:, cols].T
        cot_t[cols, ROWS:] = cot2[:, cols].T

    for cp in gathers:
        cp.wait()

    @pl.loop(0, 3)
    def _(i):
        cols = pl.ds(pl.multiple_of(i * 256, 256), 256)
        for r in range(2):
            proj[r * 256 : (r + 1) * 256, cols] = dot(normed[r * 256 : (r + 1) * 256, :], w[:, cols], 1, 0).astype(BF)

    for r, src in enumerate((cot_ref, cot2)):
        gatt[r * 256 : (r + 1) * 256, :] = dot(src[...], w[:, 3 * HALF :], 1, 0).astype(BF)

    row_at = lax.broadcasted_iota(jnp.int32, (TILE, TILE), 0)
    col_at = lax.broadcasted_iota(jnp.int32, (TILE, TILE), 1)
    causal = (row_at // CAPLEN == col_at // CAPLEN) & (col_at <= row_at)
    scale = HEAD_SIZE ** (-0.5)

    for side, real in enumerate((valid_ref, valid2)):
        @pl.loop(0, ROWS // TILE)
        def _(t):
            rows = pl.ds(pl.multiple_of(side * ROWS + t * TILE, TILE), TILE)
            keys_real = real[0:1, pl.ds(pl.multiple_of(t * TILE, TILE), TILE)]
            allowed = causal & (keys_real > 0.5)
            for h in range(4):
                q = proj[rows, h * 64 : (h + 1) * 64]
                k = proj[rows, HALF + h * 64 : HALF + (h + 1) * 64]
                v = proj[rows, 2 * HALF + h * 64 : 2 * HALF + (h + 1) * 64]
                g = gatt[rows, h * 64 : (h + 1) * 64]
                raised = jnp.where(allowed, jnp.exp(dot(q, k, 1, 1) * scale), 0.0)
                prob = raised / jnp.sum(raised, axis=-1, keepdims=True)
                rounded = prob.astype(BF)
                att[rows, h * 64 : (h + 1) * 64] = dot(rounded, v, 1, 0).astype(BF)
                grad_prob = dot(g, v, 1, 1)
                mean = jnp.sum(prob * grad_prob, axis=-1, keepdims=True)
                grad_scores = (prob * (grad_prob - mean) * scale).astype(BF)
                grads[rows, h * 64 : (h + 1) * 64] = dot(grad_scores, k, 1, 0).astype(BF)
                grads[rows, HALF + h * 64 : HALF + (h + 1) * 64] = dot(grad_scores, q, 0, 0).astype(BF)
                grads[rows, 2 * HALF + h * 64 : 2 * HALF + (h + 1) * 64] = dot(rounded, g, 0, 0).astype(BF)

    @pl.loop(0, 4)
    def _(i):
        rows = pl.ds(pl.multiple_of(i * 256, 256), 256)
        for j in range(3):
            terms[rows, j * 256 : (j + 1) * 256] = dot(normed_t[rows, :], grads[:, j * 256 : (j + 1) * 256], 1, 0).astype(BF)
        terms[rows, 3 * HALF :] = dot(cot_t[rows, :], att[...], 1, 0).astype(BF)

    def piece(tx, ty):
        return pl.ds(pl.multiple_of((ty * 4 + tx) * 64, 64), 64)

    plane = []
    for j, (dx, dy) in enumerate(PLANE):
        tx, ty = (x + dx) % NX, (y + dy) % NY
        cp = copy(terms.at[piece(tx, ty)], plane_in.at[j], p_send.at[j], p_recv.at[j], device(tx, ty, z, c))
        cp.start()
        plane.append(cp)

    @pl.loop(0, 4)
    def _(i):
        cols = pl.ds(pl.multiple_of(i * 256, 256), 256)
        mixed_out[:, cols] = dot(att[ROWS:, :], w[cols, 3 * HALF :], 1, 1).astype(BF)
        gn_out[:, cols] = dot(grads[ROWS:, :], w[cols, : 3 * HALF], 1, 1).astype(BF)

    backs = [
        copy(mixed_out, mixed_in, s_send.at[3], s_recv.at[3], sibling),
        copy(gn_out, gn_in, s_send.at[4], s_recv.at[4], sibling),
    ]
    for cp in backs:
        cp.start()

    @pl.loop(0, 4)
    def _(i):
        cols = pl.ds(pl.multiple_of(i * 256, 256), 256)
        mixed_out_own = dot(att[:ROWS, :], w[cols, 3 * HALF :], 1, 1)
        lo_ref[:, cols] = (tok_ref[:, cols].astype(F32) + mixed_out_own).astype(BF)
        gn_own[:, cols] = dot(grads[:ROWS, :], w[cols, : 3 * HALF], 1, 1)

    for cp in backs:
        cp.wait()

    @pl.loop(0, 4)
    def _(i):
        rows = pl.ds(pl.multiple_of(i * 64, 64), 64)
        floats = tok_ref[rows, :].astype(F32)
        inv = inverse[rows, 0:1]
        grad_normed = gn_own[rows, :] + gn_in[rows, :].astype(F32)
        mean = jnp.mean(grad_normed * floats, axis=-1, keepdims=True)
        gt_ref[rows, :] = (cot_ref[rows, :].astype(F32) + inv * grad_normed - floats * (inv * inv * inv * mean)).astype(BF)
        lo_ref[rows, :] = (lo_ref[rows, :].astype(F32) + mixed_in[rows, :].astype(F32)).astype(BF)

    for cp in plane:
        cp.wait()

    for rg in range(4):
        mine = pl.ds(pl.multiple_of((y * 4 + x) * 64 + rg * 16, 16), 16)
        for cg in range(4):
            cols = slice(cg * 256, (cg + 1) * 256)
            total = terms[mine, cols].astype(F32)
            for j in range(len(PLANE)):
                total = total + plane_in[j, rg * 16 : (rg + 1) * 16, cols].astype(F32)
            acc[rg * 4 + cg] = total.astype(BF)

    lines = []
    for dz in range(1, NZ):
        tz = (z + dz) % NZ
        cp = copy(acc.at[tz], z_in.at[dz - 1], z_send.at[dz - 1], z_recv.at[dz - 1], device(x, y, tz, c))
        cp.start()
        lines.append(cp)
    for cp in lines:
        cp.wait()
    total = acc[z].astype(F32)
    for j in range(NZ - 1):
        total = total + z_in[j].astype(F32)
    red[...] = total.astype(BF)
    zfin[z] = total.astype(BF)

    lines = []
    for dz in range(1, NZ):
        tz = (z + dz) % NZ
        cp = copy(red, zfin.at[z], a_send.at[dz - 1], a_recv.at[dz - 1], device(x, y, tz, c))
        cp.start()
        lines.append(cp)
    for cp in lines:
        cp.wait()

    across = copy(zfin, fin.at[c], f_send.at[0], f_recv.at[c], device(xh * 2 + 1 - xl, y, z, xl))
    beside = copy(zfin, fin.at[c], f_send.at[1], f_recv.at[c], sibling)
    across.start()

    @pl.when(c != xl)
    def _():
        beside.start()

    @pl.when(c == xl)
    def _():
        fin[c] = zfin[...]
        copy(zfin, fin.at[1 - c], f_send.at[1], f_recv.at[1 - c], sibling).wait_recv()

    @pl.when(c != xl)
    def _():
        for h in range(2):
            copy(zfin, fin.at[h], f_send.at[1], f_recv.at[h], sibling).wait_recv()
        beside.wait_send()

    across.wait_send()

    for h in range(2):
        for s in range(16):
            rg, cg = s // 4, s % 4
            rows = slice(rg * 16, (rg + 1) * 16)
            value = fin[h, s].astype(F32)
            if cg < 3:
                gin_ref[rows, cg * 512 + h * 256 : cg * 512 + (h + 1) * 256] = value
            else:
                gout_ref[rows, h * 256 : (h + 1) * 256] = value


def per_device(tokens, lengths, cotangent, input_weight, output_weight):
    real = jnp.arange(CAPLEN, dtype=jnp.int32)[None, :] < lengths[:, None]
    valid = jnp.broadcast_to(real.astype(F32).reshape(1, ROWS), (8, ROWS))
    vmem = pl.BlockSpec(memory_space=pltpu.VMEM)
    dma = pltpu.SemaphoreType.DMA
    n_g, n_p, n_z = len(GATHER), len(PLANE), NZ - 1
    return pl.pallas_call(
        kernel,
        out_shape=(
            jax.ShapeDtypeStruct((ROWS, D), BF),
            jax.ShapeDtypeStruct((ROWS, D), BF),
            jax.ShapeDtypeStruct((64, 1536), F32),
            jax.ShapeDtypeStruct((64, 512), F32),
        ),
        in_specs=[vmem] * 5,
        out_specs=(vmem,) * 4,
        scratch_shapes=[
            pltpu.VMEM((2, 64, D), BF),
            pltpu.VMEM((D, D), BF),
            pltpu.VMEM((ROWS, D), BF),
            pltpu.VMEM((ROWS, D), BF),
            pltpu.VMEM((8, ROWS), F32),
            pltpu.VMEM((2 * ROWS, D), BF),
            pltpu.VMEM((D, 2 * ROWS), BF),
            pltpu.VMEM((D, 2 * ROWS), BF),
            pltpu.VMEM((2 * ROWS, 128), F32),
            pltpu.VMEM((2 * ROWS, 3 * HALF), BF),
            pltpu.VMEM((2 * ROWS, HALF), BF),
            pltpu.VMEM((2 * ROWS, HALF), BF),
            pltpu.VMEM((2 * ROWS, 3 * HALF), BF),
            pltpu.VMEM((D, D), BF),
            pltpu.VMEM((n_p, 64, D), BF),
            pltpu.VMEM((16, 16, 256), BF),
            pltpu.VMEM((n_z, 16, 256), BF),
            pltpu.VMEM((16, 256), BF),
            pltpu.VMEM((16, 16, 256), BF),
            pltpu.VMEM((2, 16, 16, 256), BF),
            pltpu.VMEM((ROWS, D), BF),
            pltpu.VMEM((ROWS, D), BF),
            pltpu.VMEM((ROWS, D), BF),
            pltpu.VMEM((ROWS, D), BF),
            pltpu.VMEM((ROWS, D), F32),
            dma((n_g,)), dma((n_g,)),
            dma((5,)), dma((5,)),
            dma((n_p,)), dma((n_p,)),
            dma((n_z,)), dma((n_z,)),
            dma((n_z,)), dma((n_z,)),
            dma((2,)), dma((2,)),
        ],
        compiler_params=pltpu.CompilerParams(collective_id=0, has_side_effects=True, vmem_limit_bytes=50 * 2**20),
        name="layer",
    )(tokens, cotangent, valid, input_weight, output_weight)


def solution(mesh):
    placed = (
        P(("dp", "blk"), None),
        P(("dp", "blk")),
        P(("dp", "blk"), None),
        P("blk", None),
        P("blk", None),
    )
    return jax.shard_map(
        per_device,
        mesh=mesh,
        in_specs=placed,
        out_specs=(P(("dp", "blk"), None), P(("dp", "blk"), None), P("blk", None), P("blk", None)),
        check_vma=False,
    )
```

time: 541 us -> 126 us (0.23)
  the two profiles are of different devices: /device:TPU:24 before, /device:TPU:2 now
where the time goes in v1:
time: 126 us; the launch traced here: 125 us
  Pallas kernels  117 us (93%)
  local copies, waits for them, and re-layouts  6.92 us (5%)
    pallas_call x1, Pallas kernels, per_device(): pl.pallas_call(kernel, out_shape=(jax.ShapeDtypeStruct((ROWS, D), BF), ja...  117 us
    unnamed x12, local copies, waits for them, and re-layouts  6.84 us

profile of v1, /device:TPU:2, one launch (start us, length us, event | category | flops | bytes accessed | tf_op | source)
XLA Modules:
  0.0 125.3 jit_solution(12700958182126820378)
XLA Ops:
  0.6 0.7 fusion
  1.4 0.1 reshape.27
  1.4 0.0 copy-start
  1.4 1.0 copy-done
  2.5 0.0 copy-start.1
  2.5 1.0 copy-done.1
  3.5 0.0 copy-start.2
  3.5 0.9 copy-done.2
  4.5 0.0 copy-start.3
  4.5 0.8 copy-done.3
  5.3 117.0 %layer.1 = (bf16[256,1024]{1,0:T(8,128)(2,1)S(1)}, bf16[256,1024]{1,0:T(8,128)(2,1)S(1)}, f32[64,1536]{1,0:T(8,128)S(1)}, f32[64,512]{1,0:T(8,128)S(1)}) custom-call(bf16[256,1024]{1,0:T(8,128)(2,1)S(1)} %copy-done, bf16[256,1024]{1,0:T(8,128)(2,1)S(1)} %copy-done.1, f32[8,256]{1,0:T(8,128)S(1)} %broadcast_in_dim.2.valid_ref, ...), custom_call_target="tpu_custom_call" | custom-call | tf_op jit(solution)/shard_map/layer/pallas_call | solution.py:271
  122.4 0.8 copy.13
  123.1 0.8 copy.14
  123.9 0.7 copy.15
  124.7 0.7 copy.16
  (1 shorter events, 0.0 us)
Async XLA Ops:
  1.4 1.0 copy-start
  2.5 1.0 copy-start.1
  3.5 0.9 copy-start.2
  4.5 0.8 copy-start.3

commit v2 on v1

v2 whole, which is shorter than its diff:
```python
import functools

import jax
import jax.numpy as jnp
from jax import lax
from jax.experimental import pallas as pl
from jax.experimental.pallas import tpu as pltpu
from jax.sharding import PartitionSpec as P

HEADS = 8
HEAD_SIZE = 64
CAPLEN = 32
EPSILON = 1e-06

MESH = pl.DeviceIdType.MESH
NX, NY, NZ = 4, 4, 16
ROWS = 256
D = 1024
HALF = 256
TILE = 128
BF = jnp.bfloat16
F32 = jnp.float32

GATHER = [(cross, dy, dc) for cross in (0, 1) for dy in range(4) for dc in range(2) if cross or dy or dc]


def device(x, y, z, c):
    return {"dp": (x % 2) * NZ + z, "blk": y * 4 + (x // 2) * 2 + c}


def dot(a, b, ca, cb):
    return lax.dot_general(a, b, (((ca,), (cb,)), ((), ())), preferred_element_type=F32)


def kernel(
    tok_hbm, cot_hbm, valid_ref, win_hbm, wout_hbm,
    lo_ref, gt_ref, gin_ref, gout_ref,
    tok_ref, cot_ref, win_ref, wout_ref,
    stage, w, tok2, cot2, valid2, normed, normed_t, cot_t, inverse, proj, gatt, att, grads,
    terms, first_in, first_sum, second_in, acc, z_in, red, fin, mixed_out, gn_out, mixed_in, gn_in, gn_own,
    l_sem, g_send, g_recv, s_send, s_recv, p_send, p_recv, q_send, q_recv, z_send, z_recv, f_send, f_recv,
):
    dp, blk = lax.axis_index("dp"), lax.axis_index("blk")
    xl, z = dp // NZ, dp % NZ
    y, xh, c = blk // 4, (blk // 2) % 2, blk % 2
    x = xh * 2 + xl
    sibling = device(x, y, z, 1 - c)

    loads = []
    for j, (src, dst) in enumerate(((win_hbm, win_ref), (wout_hbm, wout_ref), (tok_hbm, tok_ref), (cot_hbm, cot_ref))):
        cp = pltpu.make_async_copy(src, dst, l_sem.at[j])
        cp.start()
        loads.append(cp)

    def gather_to(cross, dy, dc):
        tx = 3 - x if cross else x
        return device(tx, (y + dy) % NY, z, (c + dc) % 2), (c + dc) % 2

    barrier = pltpu.get_barrier_semaphore()
    greet = [gather_to(*o)[0] for o in GATHER]
    greet += [device((x + d) % NX, y, z, c) for d in (1, 2, 3)]
    greet += [device(xh * 2 + t, y, (z + dz) % NZ, e) for dz in range(1, NZ) for t in range(2) for e in range(2)]
    greet += [device(xh * 2 + 1 - xl, y, z, t) for t in range(2)]
    for d in greet:
        pl.semaphore_signal(barrier, inc=1, device_id=d, device_id_type=MESH)

    def copy(src, dst, ss, rs, to):
        return pltpu.make_async_remote_copy(src_ref=src, dst_ref=dst, send_sem=ss, recv_sem=rs, device_id=to, device_id_type=MESH)

    loads[0].wait()
    loads[1].wait()
    for h in range(2):
        for i in range(2):
            for part in range(3):
                at = part * 2 * HALF + h * HALF + i * 128
                stage[h, i, :, part * 128 : (part + 1) * 128] = win_ref[:, at : at + 128]
            at = h * HALF + i * 128
            stage[h, i, :, 384:] = wout_ref[:, at : at + 128]
    my_rows = pl.ds(pl.multiple_of(blk * 64, 64), 64)
    for i in range(2):
        w[i, my_rows, :] = stage[c, i]

    def normalise(src, other, at):
        @pl.loop(0, 2)
        def _(i):
            rows = pl.ds(pl.multiple_of(i * 128, 128), 128)
            out = pl.ds(pl.multiple_of(at + i * 128, 128), 128)
            floats = src[rows, :].astype(F32)
            inv = lax.rsqrt(jnp.mean(floats * floats, axis=-1, keepdims=True) + EPSILON)
            inverse[out, :] = jnp.broadcast_to(inv, (128, 128))
            normed[out, :] = (floats * inv).astype(BF)

        @pl.loop(0, 4)
        def _(i):
            cols = pl.ds(pl.multiple_of(i * 256, 256), 256)
            normed_t[cols, at : at + ROWS] = normed[at : at + ROWS, cols].T
            cot_t[cols, at : at + ROWS] = other[:, cols].T

    loads[2].wait()
    loads[3].wait()
    normalise(tok_ref, cot_ref, 0)

    pl.semaphore_wait(barrier, len(greet))

    shares = [
        copy(tok_ref, tok2, s_send.at[0], s_recv.at[0], sibling),
        copy(cot_ref, cot2, s_send.at[1], s_recv.at[1], sibling),
        copy(valid_ref, valid2, s_send.at[2], s_recv.at[2], sibling),
    ]
    for cp in shares:
        cp.start()
    gathers = []
    for i in range(2):
        for j, o in enumerate(GATHER):
            to, h = gather_to(*o)
            cp = copy(stage.at[h, i], w.at[i, my_rows], g_send.at[i, j], g_recv.at[i, j], to)
            cp.start()
            gathers.append(cp)

    for cp in shares:
        cp.wait()
    normalise(tok2, cot2, ROWS)

    row_at = lax.broadcasted_iota(jnp.int32, (TILE, TILE), 0)
    col_at = lax.broadcasted_iota(jnp.int32, (TILE, TILE), 1)
    causal = (row_at // CAPLEN == col_at // CAPLEN) & (col_at <= row_at)
    scale = HEAD_SIZE ** (-0.5)

    def attend(i):
        for r, src in enumerate((cot_ref, cot2)):
            own = slice(r * 256, (r + 1) * 256)
            proj[own, :] = dot(normed[own, :], w[i, :, :384], 1, 0).astype(BF)
            gatt[own, :] = dot(src[...], w[i, :, 384:], 1, 0).astype(BF)
        for side, real in enumerate((valid_ref, valid2)):
            @pl.loop(0, ROWS // TILE)
            def _(t):
                rows = pl.ds(pl.multiple_of(side * ROWS + t * TILE, TILE), TILE)
                keys_real = real[0:1, pl.ds(pl.multiple_of(t * TILE, TILE), TILE)]
                allowed = causal & (keys_real > 0.5)
                for h in range(2):
                    q = proj[rows, h * 64 : (h + 1) * 64]
                    k = proj[rows, 128 + h * 64 : 128 + (h + 1) * 64]
                    v = proj[rows, 256 + h * 64 : 256 + (h + 1) * 64]
                    g = gatt[rows, h * 64 : (h + 1) * 64]
                    raised = jnp.where(allowed, jnp.exp(dot(q, k, 1, 1) * scale), 0.0)
                    prob = raised / jnp.sum(raised, axis=-1, keepdims=True)
                    rounded = prob.astype(BF)
                    att[i, rows, h * 64 : (h + 1) * 64] = dot(rounded, v, 1, 0).astype(BF)
                    grad_prob = dot(g, v, 1, 1)
                    mean = jnp.sum(prob * grad_prob, axis=-1, keepdims=True)
                    grad_scores = (prob * (grad_prob - mean) * scale).astype(BF)
                    grads[i, rows, h * 64 : (h + 1) * 64] = dot(grad_scores, k, 1, 0).astype(BF)
                    grads[i, rows, 128 + h * 64 : 128 + (h + 1) * 64] = dot(grad_scores, q, 0, 0).astype(BF)
                    grads[i, rows, 256 + h * 64 : 256 + (h + 1) * 64] = dot(rounded, g, 0, 0).astype(BF)

    def products(i):
        @pl.loop(0, 4)
        def _(t):
            rows = pl.ds(pl.multiple_of(t * 256, 256), 256)
            terms[i, 0, t] = dot(normed_t[rows, :], grads[i, :, :256], 1, 0).astype(BF).reshape(4, 64, 256)
            terms[i, 1, t, :, :, :128] = dot(normed_t[rows, :], grads[i, :, 256:], 1, 0).astype(BF).reshape(4, 64, 128)
            terms[i, 1, t, :, :, 128:] = dot(cot_t[rows, :], att[i], 1, 0).astype(BF).reshape(4, 64, 128)

    def first_start(i):
        started = []
        for d in (1, 2, 3):
            tx, ty = (x + d) % NX, (y + d) % NY
            started.append(copy(terms.at[i, 0, :, tx], first_in.at[i, 0, d - 1], p_send.at[i, 0, d - 1], p_recv.at[i, 0, d - 1], device(tx, y, z, c)))
            started.append(copy(terms.at[i, 1, ty], first_in.at[i, 1, d - 1], p_send.at[i, 1, d - 1], p_recv.at[i, 1, d - 1], device(x, ty, z, c)))
        for cp in started:
            cp.start()
        return started

    def first_end(i, started):
        for cp in started:
            cp.wait()
        for g in range(4):
            for part in range(2):
                total = (terms[i, 0, g, x] if part == 0 else terms[i, 1, y, g]).astype(F32)
                for d in range(3):
                    total = total + first_in[i, part, d, g].astype(F32)
                first_sum[i, part, g] = total.astype(BF)
        started = []
        for d in (1, 2, 3):
            tx, ty = (x + d) % NX, (y + d) % NY
            started.append(copy(first_sum.at[i, 0, ty], second_in.at[i, 0, d - 1], q_send.at[i, 0, d - 1], q_recv.at[i, 0, d - 1], device(x, ty, z, c)))
            started.append(copy(first_sum.at[i, 1, tx], second_in.at[i, 1, d - 1], q_send.at[i, 1, d - 1], q_recv.at[i, 1, d - 1], device(tx, y, z, c)))
        for cp in started:
            cp.start()
        return started

    def second_end(i, started):
        for cp in started:
            cp.wait()
        for part in range(2):
            total = first_sum[i, part, y if part == 0 else x].astype(F32)
            for d in range(3):
                total = total + second_in[i, part, d].astype(F32)
            total = total.astype(BF)
            for g in range(4):
                for h in range(2):
                    acc[i, g * 4 + part * 2 + h] = total[g * 16 : (g + 1) * 16, h * 128 : (h + 1) * 128]
        started = []
        for dz in range(1, NZ):
            tz = (z + dz) % NZ
            started.append(copy(acc.at[i, tz], z_in.at[i, dz - 1], z_send.at[i, dz - 1], z_recv.at[i, dz - 1], device(x, y, tz, c)))
        for cp in started:
            cp.start()
        return started

    def line_end(i, started):
        for cp in started:
            cp.wait()
        total = acc[i, z].astype(F32)
        for j in range(NZ - 1):
            total = total + z_in[i, j].astype(F32)
        red[i] = total.astype(BF)
        started = []
        for dz in range(NZ):
            tz = (z + dz) % NZ
            for other in range(2):
                if dz or other:
                    tx = xh * 2 + (xl + other) % 2
                    started.append(copy(red.at[i], fin.at[i, c, z], f_send.at[i, dz, other], f_recv.at[i], device(tx, y, tz, xl)))
        for cp in started:
            cp.start()
        beside = copy(red.at[i], fin.at[i, c, z], f_send.at[i, 0, 0], f_recv.at[i], sibling)
        here = pltpu.make_async_copy(red.at[i], fin.at[i, c, z], f_recv.at[i])

        @pl.when(c != xl)
        def _():
            beside.start()

        @pl.when(c == xl)
        def _():
            here.start()

        return started, beside

    def back_end(i, started, beside):
        pltpu.make_async_copy(fin.at[i], fin.at[i], f_recv.at[i]).wait()
        for h in range(2):
            for s in range(16):
                rows = slice(s // 4 * 16, (s // 4 + 1) * 16)
                part = s % 4
                at = h * HALF + i * 128
                value = fin[i, h, s].astype(F32)
                if part < 3:
                    gin_ref[rows, part * 512 + at : part * 512 + at + 128] = value
                else:
                    gout_ref[rows, at : at + 128] = value
        for cp in started:
            cp.wait_send()

        @pl.when(c != xl)
        def _():
            beside.wait_send()

    for cp in gathers[: len(GATHER)]:
        cp.wait()
    attend(0)
    products(0)
    first0 = first_start(0)
    for cp in gathers[len(GATHER) :]:
        cp.wait()
    attend(1)
    products(1)
    first1 = first_start(1)
    second0 = first_end(0, first0)

    def head_sums(rows, cols):
        mixed = dot(att[0, rows, :], w[0, cols, 384:], 1, 1) + dot(att[1, rows, :], w[1, cols, 384:], 1, 1)
        back = dot(grads[0, rows, :], w[0, cols, :384], 1, 1) + dot(grads[1, rows, :], w[1, cols, :384], 1, 1)
        return mixed, back

    @pl.loop(0, 4)
    def _(t):
        cols = pl.ds(pl.multiple_of(t * 256, 256), 256)
        mixed, back = head_sums(slice(ROWS, 2 * ROWS), cols)
        mixed_out[:, cols] = mixed.astype(BF)
        gn_out[:, cols] = back.astype(BF)

    backs = [
        copy(mixed_out, mixed_in, s_send.at[3], s_recv.at[3], sibling),
        copy(gn_out, gn_in, s_send.at[4], s_recv.at[4], sibling),
    ]
    for cp in backs:
        cp.start()
    line0 = second_end(0, second0)
    second1 = first_end(1, first1)

    @pl.loop(0, 4)
    def _(t):
        cols = pl.ds(pl.multiple_of(t * 256, 256), 256)
        mixed, back = head_sums(slice(0, ROWS), cols)
        lo_ref[:, cols] = (tok_ref[:, cols].astype(F32) + mixed).astype(BF)
        gn_own[:, cols] = back

    line1 = second_end(1, second1)
    back0 = line_end(0, line0)

    for cp in backs:
        cp.wait()

    @pl.loop(0, 4)
    def _(t):
        rows = pl.ds(pl.multiple_of(t * 64, 64), 64)
        floats = tok_ref[rows, :].astype(F32)
        inv = inverse[rows, 0:1]
        grad_normed = gn_own[rows, :] + gn_in[rows, :].astype(F32)
        mean = jnp.mean(grad_normed * floats, axis=-1, keepdims=True)
        gt_ref[rows, :] = (cot_ref[rows, :].astype(F32) + inv * grad_normed - floats * (inv * inv * inv * mean)).astype(BF)
        lo_ref[rows, :] = (lo_ref[rows, :].astype(F32) + mixed_in[rows, :].astype(F32)).astype(BF)

    back1 = line_end(1, line1)
    back_end(0, *back0)
    back_end(1, *back1)


def per_device(tokens, lengths, cotangent, input_weight, output_weight):
    real = jnp.arange(CAPLEN, dtype=jnp.int32)[None, :] < lengths[:, None]
    valid = jnp.broadcast_to(real.astype(F32).reshape(1, ROWS), (8, ROWS))
    vmem, anywhere = pl.BlockSpec(memory_space=pltpu.VMEM), pl.BlockSpec(memory_space=pl.ANY)
    dma = pltpu.SemaphoreType.DMA
    n_g, n_z = len(GATHER), NZ - 1
    return pl.pallas_call(
        kernel,
        out_shape=(
            jax.ShapeDtypeStruct((ROWS, D), BF),
            jax.ShapeDtypeStruct((ROWS, D), BF),
            jax.ShapeDtypeStruct((64, 1536), F32),
            jax.ShapeDtypeStruct((64, 512), F32),
        ),
        in_specs=[anywhere, anywhere, vmem, anywhere, anywhere],
        out_specs=(vmem,) * 4,
        scratch_shapes=[
            pltpu.VMEM((ROWS, D), BF),
            pltpu.VMEM((ROWS, D), BF),
            pltpu.VMEM((64, 1536), BF),
            pltpu.VMEM((64, 512), BF),
            pltpu.VMEM((2, 2, 64, 512), BF),
            pltpu.VMEM((2, D, 512), BF),
            pltpu.VMEM((ROWS, D), BF),
            pltpu.VMEM((ROWS, D), BF),
            pltpu.VMEM((8, ROWS), F32),
            pltpu.VMEM((2 * ROWS, D), BF),
            pltpu.VMEM((D, 2 * ROWS), BF),
            pltpu.VMEM((D, 2 * ROWS), BF),
            pltpu.VMEM((2 * ROWS, 128), F32),
            pltpu.VMEM((2 * ROWS, 384), BF),
            pltpu.VMEM((2 * ROWS, 128), BF),
            pltpu.VMEM((2, 2 * ROWS, 128), BF),
            pltpu.VMEM((2, 2 * ROWS, 384), BF),
            pltpu.VMEM((2, 2, 4, 4, 64, 256), BF),
            pltpu.VMEM((2, 2, 3, 4, 64, 256), BF),
            pltpu.VMEM((2, 2, 4, 64, 256), BF),
            pltpu.VMEM((2, 2, 3, 64, 256), BF),
            pltpu.VMEM((2, 16, 16, 128), BF),
            pltpu.VMEM((2, n_z, 16, 128), BF),
            pltpu.VMEM((2, 16, 128), BF),
            pltpu.VMEM((2, 2, 16, 16, 128), BF),
            pltpu.VMEM((ROWS, D), BF),
            pltpu.VMEM((ROWS, D), BF),
            pltpu.VMEM((ROWS, D), BF),
            pltpu.VMEM((ROWS, D), BF),
            pltpu.VMEM((ROWS, D), F32),
            dma((4,)),
            dma((2, n_g)), dma((2, n_g)),
            dma((5,)), dma((5,)),
            dma((2, 2, 3)), dma((2, 2, 3)),
            dma((2, 2, 3)), dma((2, 2, 3)),
            dma((2, n_z)), dma((2, n_z)),
            dma((2, NZ, 2)), dma((2,)),
        ],
        compiler_params=pltpu.CompilerParams(collective_id=0, has_side_effects=True, vmem_limit_bytes=50 * 2**20),
        name="layer",
    )(tokens, cotangent, valid, input_weight, output_weight)


def solution(mesh):
    placed = (
        P(("dp", "blk"), None),
        P(("dp", "blk")),
        P(("dp", "blk"), None),
        P("blk", None),
        P("blk", None),
    )
    return jax.shard_map(
        per_device,
        mesh=mesh,
        in_specs=placed,
        out_specs=(P(("dp", "blk"), None), P(("dp", "blk"), None), P("blk", None), P("blk", None)),
        check_vma=False,
    )
```

time: 126 us -> 103 us (0.82)
  the two profiles are of different devices: /device:TPU:2 before, /device:TPU:1 now
where the time goes in v2:
time: 103 us; the launch traced here: 102 us
  Pallas kernels  94.2 us (91%)
  local copies, waits for them, and re-layouts  6.92 us (7%)
    pallas_call x1, Pallas kernels, per_device(): pl.pallas_call(kernel, out_shape=(jax.ShapeDtypeStruct((ROWS, D), BF), ja...  94.2 us
    unnamed x12, local copies, waits for them, and re-layouts  6.84 us

profile of v2, /device:TPU:1, one launch (start us, length us, event | category | flops | bytes accessed | tf_op | source)
XLA Modules:
  0.0 102.5 jit_solution(8226949867036237956)
XLA Ops:
  0.6 0.7 fusion
  1.4 0.1 reshape.27
  1.4 0.0 copy-start
  1.4 1.0 %copy-done = bf16[256,1024]{1,0:T(8,128)(2,1)S(1)} copy-done((bf16[256,1024]{1,0:T(8,128)(2,1)S(1)}, bf16[256,1024]{1,0:T(8,128)(2,1)}, u32[]{:S(2)}) %copy-start) | copy-done | bytes 524312
  2.5 0.0 copy-start.1
  2.5 1.0 %copy-done.1 = bf16[256,1024]{1,0:T(8,128)(2,1)S(1)} copy-done((bf16[256,1024]{1,0:T(8,128)(2,1)S(1)}, bf16[256,1024]{1,0:T(8,128)(2,1)}, u32[]{:S(2)}) %copy-start.1) | copy-done | bytes 524312
  3.5 0.0 copy-start.2
  3.5 0.9 copy-done.2
  4.5 0.0 copy-start.3
  4.5 0.8 copy-done.3
  5.3 94.2 %layer.1 = (bf16[256,1024]{1,0:T(8,128)(2,1)S(1)}, bf16[256,1024]{1,0:T(8,128)(2,1)S(1)}, f32[64,1536]{1,0:T(8,128)S(1)}, f32[64,512]{1,0:T(8,128)S(1)}) custom-call(bf16[256,1024]{1,0:T(8,128)(2,1)S(1)} %copy-done, bf16[256,1024]{1,0:T(8,128)(2,1)S(1)} %copy-done.1, f32[8,256]{1,0:T(8,128)S(1)} %broadcast_in_dim.2.valid_ref, ...), custom_call_target="tpu_custom_call" | custom-call | tf_op jit(solution)/shard_map/layer/pallas_call | solution.py:326
  99.5 0.8 copy.13
  100.3 0.8 copy.14
  101.1 0.7 copy.15
  101.8 0.7 copy.16
  (1 shorter events, 0.0 us)
Async XLA Ops:
  1.4 1.0 %copy-start = (bf16[256,1024]{1,0:T(8,128)(2,1)S(1)}, bf16[256,1024]{1,0:T(8,128)(2,1)}, u32[]{:S(2)}) copy-start(bf16[256,1024]{1,0:T(8,128)(2,1)} %tok_hbm.1) | copy-start | bytes 1572868
  2.5 1.0 %copy-start.1 = (bf16[256,1024]{1,0:T(8,128)(2,1)S(1)}, bf16[256,1024]{1,0:T(8,128)(2,1)}, u32[]{:S(2)}) copy-start(bf16[256,1024]{1,0:T(8,128)(2,1)} %cot_hbm.1) | copy-start | bytes 1572868
  3.5 0.9 copy-start.2
  4.5 0.8 copy-start.3

commit v3 on v2

--- a/solution.py
+++ b/solution.py
@@ -21,7 +21,9 @@
 BF = jnp.bfloat16
 F32 = jnp.float32
 
-GATHER = [(cross, dy, dc) for cross in (0, 1) for dy in range(4) for dc in range(2) if cross or dy or dc]
+GATHER = [(0, 1, 0), (0, 3, 0), (1, 0, 0), (0, 1, 1), (0, 3, 1), (1, 0, 1), (1, 1, 0), (1, 3, 0), (1, 1, 1), (1, 3, 1)]
+GATHER += [(0, 2, 0), (0, 2, 1), (1, 2, 0), (1, 2, 1)]
+N_G = len(GATHER)
 
 
 def device(x, y, z, c):
@@ -38,7 +40,7 @@
     tok_ref, cot_ref, win_ref, wout_ref,
     stage, w, tok2, cot2, valid2, normed, normed_t, cot_t, inverse, proj, gatt, att, grads,
     terms, first_in, first_sum, second_in, acc, z_in, red, fin, mixed_out, gn_out, mixed_in, gn_in, gn_own,
-    l_sem, g_send, g_recv, s_send, s_recv, p_send, p_recv, q_send, q_recv, z_send, z_recv, f_send, f_recv,
+    l_sem, ready, g_send, g_recv, h_send, h_recv, w_send, w_recv, s_send, s_recv, p_send, p_recv, q_send, q_recv, z_send, z_recv, f_send, f_recv,
 ):
     dp, blk = lax.axis_index("dp"), lax.axis_index("blk")
     xl, z = dp // NZ, dp % NZ
@@ -57,12 +59,19 @@
         return device(tx, (y + dy) % NY, z, (c + dc) % 2), (c + dc) % 2
 
     barrier = pltpu.get_barrier_semaphore()
-    greet = [gather_to(*o)[0] for o in GATHER]
+    greet = [gather_to(*o)[0] for o in GATHER] + [sibling]
     greet += [device((x + d) % NX, y, z, c) for d in (1, 2, 3)]
-    greet += [device(xh * 2 + t, y, (z + dz) % NZ, e) for dz in range(1, NZ) for t in range(2) for e in range(2)]
-    greet += [device(xh * 2 + 1 - xl, y, z, t) for t in range(2)]
+    greet += [device(x, y, (z + d) % NZ, c) for d in (1, NZ - 1)]
+    greet += [device(xh * 2 + 1 - xl, y, z, 1 - c)]
     for d in greet:
         pl.semaphore_signal(barrier, inc=1, device_id=d, device_id_type=MESH)
+
+    def ready_signal(k):
+        for d in (1 << k, NZ - (1 << k)):
+            pl.semaphore_signal(ready.at[k], inc=1, device_id=device(x, y, (z + d) % NZ, c), device_id_type=MESH)
+
+    def ready_wait(k):
+        pl.semaphore_wait(ready.at[k], 2)
 
     def copy(src, dst, ss, rs, to):
         return pltpu.make_async_remote_copy(src_ref=src, dst_ref=dst, send_sem=ss, recv_sem=rs, device_id=to, device_id_type=MESH)
@@ -101,57 +110,108 @@
     normalise(tok_ref, cot_ref, 0)
 
     pl.semaphore_wait(barrier, len(greet))
+    ready_signal(0)
 
     shares = [
         copy(tok_ref, tok2, s_send.at[0], s_recv.at[0], sibling),
         copy(cot_ref, cot2, s_send.at[1], s_recv.at[1], sibling),
         copy(valid_ref, valid2, s_send.at[2], s_recv.at[2], sibling),
     ]
-    for cp in shares:
-        cp.start()
-    gathers = []
-    for i in range(2):
+    colour = (z + xl + xh) % 2
+    half = pl.ds(pl.multiple_of(colour * 32, 32), 32)
+    my_half = pl.ds(pl.multiple_of(blk * 64 + colour * 32, 32), 32)
+    hand_to = [device(x, y, (z + 1) % NZ, c), device(x, y, (z + NZ - 1) % NZ, c), device(xh * 2 + 1 - xl, y, z, c)]
+
+    def direct_start(i):
+        started = []
         for j, o in enumerate(GATHER):
             to, h = gather_to(*o)
-            cp = copy(stage.at[h, i], w.at[i, my_rows], g_send.at[i, j], g_recv.at[i, j], to)
+            started.append(copy(stage.at[h, i, half], w.at[i, my_half], g_send.at[i, j], g_recv.at[i, j], to))
+        for cp in started:
             cp.start()
-            gathers.append(cp)
-
+        return started
+
+    def hand_start(i, j):
+        cross, dy, dc = GATHER[j]
+        block = (y + NY - dy) % NY * 4 + (1 - xh if cross else xh) * 2 + (c + dc) % 2
+        rows = pl.ds(pl.multiple_of(block * 64 + colour * 32, 32), 32)
+        cp = copy(w.at[i, rows], w.at[i, rows], h_send.at[i, j], h_recv.at[i, j], hand_to[j % 3])
+        cp.start()
+        return cp
+
+    wides = [copy(stage.at[1 - c, i], w.at[i, my_rows], w_send.at[i], w_recv.at[i], sibling) for i in range(2)]
+    direct0 = direct_start(0)
+    shares[0].start()
+    shares[1].start()
+    shares[2].start()
+    wides[0].start()
+    wides[1].start()
     for cp in shares:
         cp.wait()
+    ready_wait(0)
+    ready_signal(1)
+    hands0 = []
+    for j in range(6):
+        direct0[j].wait_recv()
+        hands0.append(hand_start(0, j))
+    direct1 = direct_start(1)
+    for j in range(6, N_G):
+        direct0[j].wait_recv()
+        hands0.append(hand_start(0, j))
     normalise(tok2, cot2, ROWS)
+    ready_wait(1)
+    ready_signal(2)
+
+    def gather_end(i, hands):
+        for cp in hands:
+            cp.wait_recv()
+        wides[i].wait_recv()
 
     row_at = lax.broadcasted_iota(jnp.int32, (TILE, TILE), 0)
     col_at = lax.broadcasted_iota(jnp.int32, (TILE, TILE), 1)
     causal = (row_at // CAPLEN == col_at // CAPLEN) & (col_at <= row_at)
     scale = HEAD_SIZE ** (-0.5)
 
-    def attend(i):
+    first_head = lax.broadcasted_iota(jnp.int32, (TILE, 128), 1) < HEAD_SIZE
+
+    def stack(pair):
+        zero = jnp.zeros_like(pair)
+        return jnp.concatenate([jnp.where(first_head, pair, zero), jnp.where(first_head, zero, pair)], axis=0)
+
+    def unstack(both):
+        return jnp.where(first_head, both[:TILE], both[TILE:])
+
+    def project(i):
         for r, src in enumerate((cot_ref, cot2)):
             own = slice(r * 256, (r + 1) * 256)
             proj[own, :] = dot(normed[own, :], w[i, :, :384], 1, 0).astype(BF)
             gatt[own, :] = dot(src[...], w[i, :, 384:], 1, 0).astype(BF)
-        for side, real in enumerate((valid_ref, valid2)):
-            @pl.loop(0, ROWS // TILE)
-            def _(t):
-                rows = pl.ds(pl.multiple_of(side * ROWS + t * TILE, TILE), TILE)
-                keys_real = real[0:1, pl.ds(pl.multiple_of(t * TILE, TILE), TILE)]
-                allowed = causal & (keys_real > 0.5)
-                for h in range(2):
-                    q = proj[rows, h * 64 : (h + 1) * 64]
-                    k = proj[rows, 128 + h * 64 : 128 + (h + 1) * 64]
-                    v = proj[rows, 256 + h * 64 : 256 + (h + 1) * 64]
-                    g = gatt[rows, h * 64 : (h + 1) * 64]
-                    raised = jnp.where(allowed, jnp.exp(dot(q, k, 1, 1) * scale), 0.0)
-                    prob = raised / jnp.sum(raised, axis=-1, keepdims=True)
-                    rounded = prob.astype(BF)
-                    att[i, rows, h * 64 : (h + 1) * 64] = dot(rounded, v, 1, 0).astype(BF)
-                    grad_prob = dot(g, v, 1, 1)
-                    mean = jnp.sum(prob * grad_prob, axis=-1, keepdims=True)
-                    grad_scores = (prob * (grad_prob - mean) * scale).astype(BF)
-                    grads[i, rows, h * 64 : (h + 1) * 64] = dot(grad_scores, k, 1, 0).astype(BF)
-                    grads[i, rows, 128 + h * 64 : 128 + (h + 1) * 64] = dot(grad_scores, q, 0, 0).astype(BF)
-                    grads[i, rows, 256 + h * 64 : 256 + (h + 1) * 64] = dot(rounded, g, 0, 0).astype(BF)
+
+    def attend(i):
+        tiles = [(side, t) for side in range(2) for t in range(ROWS // TILE)]
+        rows = [slice(side * ROWS + t * TILE, side * ROWS + (t + 1) * TILE) for side, t in tiles]
+        q = [stack(proj[r, :128]) for r in rows]
+        k = [proj[r, 128:256] for r in rows]
+        v = [proj[r, 256:] for r in rows]
+        g = [stack(gatt[r, :]) for r in rows]
+        scores = [dot(a, b, 1, 1) for a, b in zip(q, k)]
+        grad_prob = [dot(a, b, 1, 1) for a, b in zip(g, v)]
+        raised = []
+        for (side, t), sc in zip(tiles, scores):
+            keys_real = (valid_ref, valid2)[side][0:1, t * TILE : (t + 1) * TILE]
+            allowed = causal & (keys_real > 0.5)
+            raised.append(jnp.where(jnp.concatenate([allowed, allowed], axis=0), jnp.exp(sc * scale), 0.0))
+        prob = [e / jnp.sum(e, axis=-1, keepdims=True) for e in raised]
+        rounded = [p.astype(BF) for p in prob]
+        for r, p, b in zip(rows, rounded, v):
+            att[i, r, :] = unstack(dot(p, b, 1, 0)).astype(BF)
+        for r, p, b in zip(rows, rounded, g):
+            grads[i, r, 256:] = dot(p, b, 0, 0).astype(BF)
+        grad_scores = [(p * (gp - jnp.sum(p * gp, axis=-1, keepdims=True)) * scale).astype(BF) for p, gp in zip(prob, grad_prob)]
+        for r, gs, b in zip(rows, grad_scores, k):
+            grads[i, r, :128] = unstack(dot(gs, b, 1, 0)).astype(BF)
+        for r, gs, b in zip(rows, grad_scores, q):
+            grads[i, r, 128:256] = dot(gs, b, 0, 0).astype(BF)
 
     def products(i):
         @pl.loop(0, 4)
@@ -256,17 +316,22 @@
         def _():
             beside.wait_send()
 
-    for cp in gathers[: len(GATHER)]:
-        cp.wait()
+    gather_end(0, hands0)
+    project(0)
+    hands1 = []
+    for j in range(N_G):
+        direct1[j].wait_recv()
+        hands1.append(hand_start(1, j))
     attend(0)
     products(0)
     first0 = first_start(0)
-    for cp in gathers[len(GATHER) :]:
-        cp.wait()
+    gather_end(1, hands1)
+    project(1)
     attend(1)
     products(1)
     first1 = first_start(1)
     second0 = first_end(0, first0)
+    ready_wait(2)
 
     def head_sums(rows, cols):
         mixed = dot(att[0, rows, :], w[0, cols, 384:], 1, 1) + dot(att[1, rows, :], w[1, cols, 384:], 1, 1)
@@ -315,14 +380,16 @@
     back1 = line_end(1, line1)
     back_end(0, *back0)
     back_end(1, *back1)
+    for cp in direct0 + direct1 + hands0 + hands1 + wides:
+        cp.wait_send()
 
 
 def per_device(tokens, lengths, cotangent, input_weight, output_weight):
     real = jnp.arange(CAPLEN, dtype=jnp.int32)[None, :] < lengths[:, None]
     valid = jnp.broadcast_to(real.astype(F32).reshape(1, ROWS), (8, ROWS))
-    vmem, anywhere = pl.BlockSpec(memory_space=pltpu.VMEM), pl.BlockSpec(memory_space=pl.ANY)
+    vmem, hbm = pl.BlockSpec(memory_space=pltpu.VMEM), pl.BlockSpec(memory_space=pltpu.HBM)
     dma = pltpu.SemaphoreType.DMA
-    n_g, n_z = len(GATHER), NZ - 1
+    n_z = NZ - 1
     return pl.pallas_call(
         kernel,
         out_shape=(
@@ -331,7 +398,7 @@
             jax.ShapeDtypeStruct((64, 1536), F32),
             jax.ShapeDtypeStruct((64, 512), F32),
         ),
-        in_specs=[anywhere, anywhere, vmem, anywhere, anywhere],
+        in_specs=[hbm, hbm, vmem, hbm, hbm],
         out_specs=(vmem,) * 4,
         scratch_shapes=[
             pltpu.VMEM((ROWS, D), BF),
@@ -365,7 +432,10 @@
             pltpu.VMEM((ROWS, D), BF),
             pltpu.VMEM((ROWS, D), F32),
             dma((4,)),
-            dma((2, n_g)), dma((2, n_g)),
+            pltpu.SemaphoreType.REGULAR((3,)),
+            dma((2, N_G)), dma((2, N_G)),
+            dma((2, N_G)), dma((2, N_G)),
+            dma((2,)), dma((2,)),
             dma((5,)), dma((5,)),
             dma((2, 2, 3)), dma((2, 2, 3)),
             dma((2, 2, 3)), dma((2, 2, 3)),

time: 103 us -> 81.5 us (0.79)
  Pallas kernels: 94.2 us -> 73 us
    pallas_call x1, Pallas kernels: 94.2 us -> 73 us  [per_device(): pl.pallas_call(kernel, out_shape=(jax.ShapeDtypeStruct((ROWS, D), BF), ja...]
where the time goes in v3:
time: 81.5 us; the launch traced here: 81.3 us
  Pallas kernels  73 us (90%)
  local copies, waits for them, and re-layouts  6.92 us (8%)
    pallas_call x1, Pallas kernels, per_device(): pl.pallas_call(kernel, out_shape=(jax.ShapeDtypeStruct((ROWS, D), BF), ja...  73 us
    unnamed x12, local copies, waits for them, and re-layouts  6.84 us

profile of v3, /device:TPU:1, one launch (start us, length us, event | category | flops | bytes accessed | tf_op | source)
XLA Modules:
  0.0 81.3 jit_solution(14760631337370835270)
XLA Ops:
  0.6 0.7 fusion
  1.4 0.1 reshape.27
  1.4 0.0 copy-start
  1.4 1.0 %copy-done = bf16[256,1024]{1,0:T(8,128)(2,1)S(1)} copy-done((bf16[256,1024]{1,0:T(8,128)(2,1)S(1)}, bf16[256,1024]{1,0:T(8,128)(2,1)}, u32[]{:S(2)}) %copy-start) | copy-done | bytes 524312
  2.5 0.0 copy-start.1
  2.5 1.0 %copy-done.1 = bf16[256,1024]{1,0:T(8,128)(2,1)S(1)} copy-done((bf16[256,1024]{1,0:T(8,128)(2,1)S(1)}, bf16[256,1024]{1,0:T(8,128)(2,1)}, u32[]{:S(2)}) %copy-start.1) | copy-done | bytes 524312
  3.5 0.0 copy-start.2
  3.5 0.9 %copy-done.2 = bf16[64,1536]{1,0:T(8,128)(2,1)S(1)} copy-done((bf16[64,1536]{1,0:T(8,128)(2,1)S(1)}, bf16[64,1536]{1,0:T(8,128)(2,1)}, u32[]{:S(2)}) %copy-start.2) | copy-done | bytes 196632
  4.5 0.0 copy-start.3
  4.5 0.8 %copy-done.3 = bf16[64,512]{1,0:T(8,128)(2,1)S(1)} copy-done((bf16[64,512]{1,0:T(8,128)(2,1)S(1)}, bf16[64,512]{1,0:T(8,128)(2,1)}, u32[]{:S(2)}) %copy-start.3) | copy-done | bytes 65560
  5.3 73.0 %layer.1 = (bf16[256,1024]{1,0:T(8,128)(2,1)S(1)}, bf16[256,1024]{1,0:T(8,128)(2,1)S(1)}, f32[64,1536]{1,0:T(8,128)S(1)}, f32[64,512]{1,0:T(8,128)S(1)}) custom-call(bf16[256,1024]{1,0:T(8,128)(2,1)S(1)} %copy-done, bf16[256,1024]{1,0:T(8,128)(2,1)S(1)} %copy-done.1, f32[8,256]{1,0:T(8,128)S(1)} %broadcast_in_dim.2.valid_ref, ...), custom_call_target="tpu_custom_call" | custom-call | tf_op jit(solution)/shard_map/layer/pallas_call | solution.py:393
  78.3 0.8 copy.13
  79.1 0.8 copy.14
  79.9 0.7 copy.15
  80.6 0.7 copy.16
  (1 shorter events, 0.0 us)
Async XLA Ops:
  1.4 1.0 %copy-start = (bf16[256,1024]{1,0:T(8,128)(2,1)S(1)}, bf16[256,1024]{1,0:T(8,128)(2,1)}, u32[]{:S(2)}) copy-start(bf16[256,1024]{1,0:T(8,128)(2,1)} %tok_hbm.1) | copy-start | bytes 1572868
  2.5 1.0 %copy-start.1 = (bf16[256,1024]{1,0:T(8,128)(2,1)S(1)}, bf16[256,1024]{1,0:T(8,128)(2,1)}, u32[]{:S(2)}) copy-start(bf16[256,1024]{1,0:T(8,128)(2,1)} %cot_hbm.1) | copy-start | bytes 1572868
  3.5 0.9 %copy-start.2 = (bf16[64,1536]{1,0:T(8,128)(2,1)S(1)}, bf16[64,1536]{1,0:T(8,128)(2,1)}, u32[]{:S(2)}) copy-start(bf16[64,1536]{1,0:T(8,128)(2,1)} %win_hbm.1) | copy-start | bytes 589828
  4.5 0.8 %copy-start.3 = (bf16[64,512]{1,0:T(8,128)(2,1)S(1)}, bf16[64,512]{1,0:T(8,128)(2,1)}, u32[]{:S(2)}) copy-start(bf16[64,512]{1,0:T(8,128)(2,1)} %wout_hbm.1) | copy-start | bytes 196612

commit v4 on v3

--- a/solution.py
+++ b/solution.py
@@ -35,12 +35,12 @@
 
 
 def kernel(
-    tok_hbm, cot_hbm, valid_ref, win_hbm, wout_hbm,
-    lo_ref, gt_ref, gin_ref, gout_ref,
-    tok_ref, cot_ref, win_ref, wout_ref,
-    stage, w, tok2, cot2, valid2, normed, normed_t, cot_t, inverse, proj, gatt, att, grads,
+    tok_hbm, cot_hbm, lengths_ref, win_hbm, wout_hbm,
+    lo_hbm, gt_hbm, gin_hbm, gout_hbm,
+    lo_ref, gt_ref, gin_ref, gout_ref, lens, tok_ref, cot_ref, win_ref, wout_ref,
+    stage, w, tok2, cot2, lens2, normed, normed_t, cot_t, inverse, proj, gatt, att, grads, probs,
     terms, first_in, first_sum, second_in, acc, z_in, red, fin, mixed_out, gn_out, mixed_in, gn_in, gn_own,
-    l_sem, ready, g_send, g_recv, h_send, h_recv, w_send, w_recv, s_send, s_recv, p_send, p_recv, q_send, q_recv, z_send, z_recv, f_send, f_recv,
+    l_sem, o_sem, ready, g_send, g_recv, h_send, h_recv, w_send, w_recv, s_send, s_recv, p_send, p_recv, q_send, q_recv, z_send, z_recv, f_send, f_recv,
 ):
     dp, blk = lax.axis_index("dp"), lax.axis_index("blk")
     xl, z = dp // NZ, dp % NZ
@@ -75,6 +75,12 @@
 
     def copy(src, dst, ss, rs, to):
         return pltpu.make_async_remote_copy(src_ref=src, dst_ref=dst, send_sem=ss, recv_sem=rs, device_id=to, device_id_type=MESH)
+
+    caption = lax.broadcasted_iota(jnp.int32, (8, ROWS), 1) // CAPLEN
+    held = jnp.zeros((8, ROWS), F32)
+    for n in range(ROWS // CAPLEN):
+        held = jnp.where(caption == n, lengths_ref[n].astype(F32), held)
+    lens[...] = held
 
     loads[0].wait()
     loads[1].wait()
@@ -105,17 +111,13 @@
             normed_t[cols, at : at + ROWS] = normed[at : at + ROWS, cols].T
             cot_t[cols, at : at + ROWS] = other[:, cols].T
 
-    loads[2].wait()
-    loads[3].wait()
-    normalise(tok_ref, cot_ref, 0)
-
     pl.semaphore_wait(barrier, len(greet))
     ready_signal(0)
 
     shares = [
         copy(tok_ref, tok2, s_send.at[0], s_recv.at[0], sibling),
         copy(cot_ref, cot2, s_send.at[1], s_recv.at[1], sibling),
-        copy(valid_ref, valid2, s_send.at[2], s_recv.at[2], sibling),
+        copy(lens, lens2, s_send.at[2], s_recv.at[2], sibling),
     ]
     colour = (z + xl + xh) % 2
     half = pl.ds(pl.multiple_of(colour * 32, 32), 32)
@@ -141,13 +143,14 @@
 
     wides = [copy(stage.at[1 - c, i], w.at[i, my_rows], w_send.at[i], w_recv.at[i], sibling) for i in range(2)]
     direct0 = direct_start(0)
+    loads[2].wait()
+    loads[3].wait()
     shares[0].start()
     shares[1].start()
     shares[2].start()
     wides[0].start()
     wides[1].start()
-    for cp in shares:
-        cp.wait()
+    normalise(tok_ref, cot_ref, 0)
     ready_wait(0)
     ready_signal(1)
     hands0 = []
@@ -158,6 +161,8 @@
     for j in range(6, N_G):
         direct0[j].wait_recv()
         hands0.append(hand_start(0, j))
+    for cp in shares:
+        cp.wait()
     normalise(tok2, cot2, ROWS)
     ready_wait(1)
     ready_signal(2)
@@ -167,12 +172,14 @@
             cp.wait_recv()
         wides[i].wait_recv()
 
-    row_at = lax.broadcasted_iota(jnp.int32, (TILE, TILE), 0)
-    col_at = lax.broadcasted_iota(jnp.int32, (TILE, TILE), 1)
-    causal = (row_at // CAPLEN == col_at // CAPLEN) & (col_at <= row_at)
+    key_at = lax.broadcasted_iota(jnp.int32, (TILE, 2 * TILE), 0)
+    query_at = lax.broadcasted_iota(jnp.int32, (TILE, 2 * TILE), 1) % TILE
+    causal = (key_at // CAPLEN == query_at // CAPLEN) & (key_at <= query_at)
+    key_place = (key_at % CAPLEN).astype(F32)
     scale = HEAD_SIZE ** (-0.5)
-
     first_head = lax.broadcasted_iota(jnp.int32, (TILE, 128), 1) < HEAD_SIZE
+    tiles = [(side, t) for side in range(2) for t in range(ROWS // TILE)]
+    tile_rows = [slice(side * ROWS + t * TILE, side * ROWS + (t + 1) * TILE) for side, t in tiles]
 
     def stack(pair):
         zero = jnp.zeros_like(pair)
@@ -188,63 +195,74 @@
             gatt[own, :] = dot(src[...], w[i, :, 384:], 1, 0).astype(BF)
 
     def attend(i):
-        tiles = [(side, t) for side in range(2) for t in range(ROWS // TILE)]
-        rows = [slice(side * ROWS + t * TILE, side * ROWS + (t + 1) * TILE) for side, t in tiles]
-        q = [stack(proj[r, :128]) for r in rows]
-        k = [proj[r, 128:256] for r in rows]
-        v = [proj[r, 256:] for r in rows]
-        g = [stack(gatt[r, :]) for r in rows]
-        scores = [dot(a, b, 1, 1) for a, b in zip(q, k)]
-        grad_prob = [dot(a, b, 1, 1) for a, b in zip(g, v)]
+        scores = [dot(proj[r, 128:256], stack(proj[r, :128]), 1, 1) for r in tile_rows]
         raised = []
         for (side, t), sc in zip(tiles, scores):
-            keys_real = (valid_ref, valid2)[side][0:1, t * TILE : (t + 1) * TILE]
-            allowed = causal & (keys_real > 0.5)
-            raised.append(jnp.where(jnp.concatenate([allowed, allowed], axis=0), jnp.exp(sc * scale), 0.0))
-        prob = [e / jnp.sum(e, axis=-1, keepdims=True) for e in raised]
+            real = (lens, lens2)[side][0:1, t * TILE : (t + 1) * TILE]
+            allowed = causal & (key_place < jnp.concatenate([real, real], axis=1))
+            raised.append(jnp.where(allowed, jnp.exp(sc * scale), 0.0))
+        prob = [e / jnp.sum(e, axis=0, keepdims=True) for e in raised]
+        for n, p in enumerate(prob):
+            probs[n] = p
         rounded = [p.astype(BF) for p in prob]
-        for r, p, b in zip(rows, rounded, v):
-            att[i, r, :] = unstack(dot(p, b, 1, 0)).astype(BF)
-        for r, p, b in zip(rows, rounded, g):
-            grads[i, r, 256:] = dot(p, b, 0, 0).astype(BF)
-        grad_scores = [(p * (gp - jnp.sum(p * gp, axis=-1, keepdims=True)) * scale).astype(BF) for p, gp in zip(prob, grad_prob)]
-        for r, gs, b in zip(rows, grad_scores, k):
-            grads[i, r, :128] = unstack(dot(gs, b, 1, 0)).astype(BF)
-        for r, gs, b in zip(rows, grad_scores, q):
-            grads[i, r, 128:256] = dot(gs, b, 0, 0).astype(BF)
-
-    def products(i):
+        for r, p in zip(tile_rows, rounded):
+            grads[i, r, 256:] = dot(p, stack(gatt[r, :]), 1, 0).astype(BF)
+        for r, p in zip(tile_rows, rounded):
+            att[i, r, :] = unstack(dot(p, proj[r, 256:], 0, 0)).astype(BF)
+
+    def attend_back(i):
+        grad_prob = [dot(proj[r, 256:], stack(gatt[r, :]), 1, 1) for r in tile_rows]
+        grad_scores = []
+        for n, gp in enumerate(grad_prob):
+            p = probs[n]
+            grad_scores.append((p * (gp - jnp.sum(p * gp, axis=0, keepdims=True)) * scale).astype(BF))
+        for r, gs in zip(tile_rows, grad_scores):
+            grads[i, r, 128:256] = dot(gs, stack(proj[r, :128]), 1, 0).astype(BF)
+        for r, gs in zip(tile_rows, grad_scores):
+            grads[i, r, :128] = unstack(dot(gs, proj[r, 128:256], 0, 0)).astype(BF)
+
+    def products_values(i):
         @pl.loop(0, 4)
         def _(t):
             rows = pl.ds(pl.multiple_of(t * 256, 256), 256)
-            terms[i, 0, t] = dot(normed_t[rows, :], grads[i, :, :256], 1, 0).astype(BF).reshape(4, 64, 256)
-            terms[i, 1, t, :, :, :128] = dot(normed_t[rows, :], grads[i, :, 256:], 1, 0).astype(BF).reshape(4, 64, 128)
-            terms[i, 1, t, :, :, 128:] = dot(cot_t[rows, :], att[i], 1, 0).astype(BF).reshape(4, 64, 128)
-
-    def first_start(i):
+            terms[i, 2, t] = dot(normed_t[rows, :], grads[i, :, 256:], 1, 0).astype(BF).reshape(4, 64, 128)
+            terms[i, 3, t] = dot(cot_t[rows, :], att[i], 1, 0).astype(BF).reshape(4, 64, 128)
+
+    def products_scores(i):
+        @pl.loop(0, 4)
+        def _(t):
+            rows = pl.ds(pl.multiple_of(t * 256, 256), 256)
+            both = dot(normed_t[rows, :], grads[i, :, :256], 1, 0).astype(BF)
+            terms[i, 0, t] = both[:, :128].reshape(4, 64, 128)
+            terms[i, 1, t] = both[:, 128:].reshape(4, 64, 128)
+
+    def first_start(i, groups):
         started = []
         for d in (1, 2, 3):
             tx, ty = (x + d) % NX, (y + d) % NY
-            started.append(copy(terms.at[i, 0, :, tx], first_in.at[i, 0, d - 1], p_send.at[i, 0, d - 1], p_recv.at[i, 0, d - 1], device(tx, y, z, c)))
-            started.append(copy(terms.at[i, 1, ty], first_in.at[i, 1, d - 1], p_send.at[i, 1, d - 1], p_recv.at[i, 1, d - 1], device(x, ty, z, c)))
+            for g in groups:
+                src = terms.at[i, g, ty] if g % 2 else terms.at[i, g, :, tx]
+                to = device(x, ty, z, c) if g % 2 else device(tx, y, z, c)
+                started.append(copy(src, first_in.at[i, g, d - 1], p_send.at[i, g, d - 1], p_recv.at[i, g, d - 1], to))
         for cp in started:
             cp.start()
         return started
 
-    def first_end(i, started):
+    def first_end(i, groups, started):
         for cp in started:
             cp.wait()
-        for g in range(4):
-            for part in range(2):
-                total = (terms[i, 0, g, x] if part == 0 else terms[i, 1, y, g]).astype(F32)
+        for g in groups:
+            for n in range(4):
+                total = (terms[i, g, y, n] if g % 2 else terms[i, g, n, x]).astype(F32)
                 for d in range(3):
-                    total = total + first_in[i, part, d, g].astype(F32)
-                first_sum[i, part, g] = total.astype(BF)
+                    total = total + first_in[i, g, d, n].astype(F32)
+                first_sum[i, g, n] = total.astype(BF)
         started = []
         for d in (1, 2, 3):
             tx, ty = (x + d) % NX, (y + d) % NY
-            started.append(copy(first_sum.at[i, 0, ty], second_in.at[i, 0, d - 1], q_send.at[i, 0, d - 1], q_recv.at[i, 0, d - 1], device(x, ty, z, c)))
-            started.append(copy(first_sum.at[i, 1, tx], second_in.at[i, 1, d - 1], q_send.at[i, 1, d - 1], q_recv.at[i, 1, d - 1], device(tx, y, z, c)))
+            for g in groups:
+                to = device(tx, y, z, c) if g % 2 else device(x, ty, z, c)
+                started.append(copy(first_sum.at[i, g, tx if g % 2 else ty], second_in.at[i, g, d - 1], q_send.at[i, g, d - 1], q_recv.at[i, g, d - 1], to))
         for cp in started:
             cp.start()
         return started
@@ -252,14 +270,13 @@
     def second_end(i, started):
         for cp in started:
             cp.wait()
-        for part in range(2):
-            total = first_sum[i, part, y if part == 0 else x].astype(F32)
+        for g in range(4):
+            total = first_sum[i, g, x if g % 2 else y].astype(F32)
             for d in range(3):
-                total = total + second_in[i, part, d].astype(F32)
+                total = total + second_in[i, g, d].astype(F32)
             total = total.astype(BF)
-            for g in range(4):
-                for h in range(2):
-                    acc[i, g * 4 + part * 2 + h] = total[g * 16 : (g + 1) * 16, h * 128 : (h + 1) * 128]
+            for n in range(4):
+                acc[i, n * 4 + g] = total[n * 16 : (n + 1) * 16]
         started = []
         for dz in range(1, NZ):
             tz = (z + dz) % NZ
@@ -297,7 +314,7 @@
 
         return started, beside
 
-    def back_end(i, started, beside):
+    def back_end(i):
         pltpu.make_async_copy(fin.at[i], fin.at[i], f_recv.at[i]).wait()
         for h in range(2):
             for s in range(16):
@@ -309,6 +326,8 @@
                     gin_ref[rows, part * 512 + at : part * 512 + at + 128] = value
                 else:
                     gout_ref[rows, at : at + 128] = value
+
+    def back_sent(started, beside):
         for cp in started:
             cp.wait_send()
 
@@ -316,6 +335,7 @@
         def _():
             beside.wait_send()
 
+    values, score_groups = (2, 3), (0, 1)
     gather_end(0, hands0)
     project(0)
     hands1 = []
@@ -323,14 +343,21 @@
         direct1[j].wait_recv()
         hands1.append(hand_start(1, j))
     attend(0)
-    products(0)
-    first0 = first_start(0)
+    products_values(0)
+    first0v = first_start(0, values)
+    attend_back(0)
+    products_scores(0)
+    first0s = first_start(0, score_groups)
     gather_end(1, hands1)
     project(1)
     attend(1)
-    products(1)
-    first1 = first_start(1)
-    second0 = first_end(0, first0)
+    products_values(1)
+    first1v = first_start(1, values)
+    second0v = first_end(0, values, first0v)
+    attend_back(1)
+    products_scores(1)
+    first1s = first_start(1, score_groups)
+    second0s = first_end(0, score_groups, first0s)
     ready_wait(2)
 
     def head_sums(rows, cols):
@@ -351,8 +378,8 @@
     ]
     for cp in backs:
         cp.start()
-    line0 = second_end(0, second0)
-    second1 = first_end(1, first1)
+    second1v = first_end(1, values, first1v)
+    line0 = second_end(0, second0v + second0s)
 
     @pl.loop(0, 4)
     def _(t):
@@ -361,7 +388,8 @@
         lo_ref[:, cols] = (tok_ref[:, cols].astype(F32) + mixed).astype(BF)
         gn_own[:, cols] = back
 
-    line1 = second_end(1, second1)
+    second1s = first_end(1, score_groups, first1s)
+    line1 = second_end(1, second1v + second1s)
     back0 = line_end(0, line0)
 
     for cp in backs:
@@ -377,30 +405,62 @@
         gt_ref[rows, :] = (cot_ref[rows, :].astype(F32) + inv * grad_normed - floats * (inv * inv * inv * mean)).astype(BF)
         lo_ref[rows, :] = (lo_ref[rows, :].astype(F32) + mixed_in[rows, :].astype(F32)).astype(BF)
 
+    outs = [
+        pltpu.make_async_copy(lo_ref, lo_hbm, o_sem.at[0]),
+        pltpu.make_async_copy(gt_ref, gt_hbm, o_sem.at[1]),
+        pltpu.make_async_copy(gin_ref, gin_hbm, o_sem.at[2]),
+        pltpu.make_async_copy(gout_ref, gout_hbm, o_sem.at[3]),
+    ]
+    outs[0].start()
+    outs[1].start()
     back1 = line_end(1, line1)
-    back_end(0, *back0)
-    back_end(1, *back1)
+    back_end(0)
+    back_end(1)
+    outs[2].start()
+    outs[3].start()
+    back_sent(*back0)
+    back_sent(*back1)
     for cp in direct0 + direct1 + hands0 + hands1 + wides:
         cp.wait_send()
+    for cp in outs:
+        cp.wait()
+
+
+def hand_over(*refs):
+    sems = refs[-1]
+    here = refs[8:12]
+    loads = [pltpu.make_async_copy(src, mid, sems.at[0, j]) for j, (src, mid) in enumerate(zip(refs[:4], here))]
+    stores = [pltpu.make_async_copy(mid, dst, sems.at[1, j]) for j, (mid, dst) in enumerate(zip(here, refs[4:8]))]
+    for cp in loads:
+        cp.start()
+    for load, store in zip(loads, stores):
+        load.wait()
+        store.start()
+    for cp in stores:
+        cp.wait()
 
 
 def per_device(tokens, lengths, cotangent, input_weight, output_weight):
-    real = jnp.arange(CAPLEN, dtype=jnp.int32)[None, :] < lengths[:, None]
-    valid = jnp.broadcast_to(real.astype(F32).reshape(1, ROWS), (8, ROWS))
-    vmem, hbm = pl.BlockSpec(memory_space=pltpu.VMEM), pl.BlockSpec(memory_space=pltpu.HBM)
+    hbm, smem = pl.BlockSpec(memory_space=pl.ANY), pl.BlockSpec(memory_space=pltpu.SMEM)
     dma = pltpu.SemaphoreType.DMA
     n_z = NZ - 1
-    return pl.pallas_call(
+    shapes = (
+        jax.ShapeDtypeStruct((ROWS, D), BF),
+        jax.ShapeDtypeStruct((ROWS, D), BF),
+        jax.ShapeDtypeStruct((64, 1536), F32),
+        jax.ShapeDtypeStruct((64, 512), F32),
+    )
+    made = pl.pallas_call(
         kernel,
-        out_shape=(
-            jax.ShapeDtypeStruct((ROWS, D), BF),
-            jax.ShapeDtypeStruct((ROWS, D), BF),
-            jax.ShapeDtypeStruct((64, 1536), F32),
-            jax.ShapeDtypeStruct((64, 512), F32),
-        ),
-        in_specs=[hbm, hbm, vmem, hbm, hbm],
-        out_specs=(vmem,) * 4,
+        out_shape=shapes,
+        in_specs=[hbm, hbm, smem, hbm, hbm],
+        out_specs=(hbm,) * 4,
         scratch_shapes=[
+            pltpu.VMEM((ROWS, D), BF),
+            pltpu.VMEM((ROWS, D), BF),
+            pltpu.VMEM((64, 1536), F32),
+            pltpu.VMEM((64, 512), F32),
+            pltpu.VMEM((8, ROWS), F32),
             pltpu.VMEM((ROWS, D), BF),
             pltpu.VMEM((ROWS, D), BF),
             pltpu.VMEM((64, 1536), BF),
@@ -418,10 +478,11 @@
             pltpu.VMEM((2 * ROWS, 128), BF),
             pltpu.VMEM((2, 2 * ROWS, 128), BF),
             pltpu.VMEM((2, 2 * ROWS, 384), BF),
-            pltpu.VMEM((2, 2, 4, 4, 64, 256), BF),
-            pltpu.VMEM((2, 2, 3, 4, 64, 256), BF),
-            pltpu.VMEM((2, 2, 4, 64, 256), BF),
-            pltpu.VMEM((2, 2, 3, 64, 256), BF),
+            pltpu.VMEM((4, TILE, 2 * TILE), F32),
+            pltpu.VMEM((2, 4, 4, 4, 64, 128), BF),
+            pltpu.VMEM((2, 4, 3, 4, 64, 128), BF),
+            pltpu.VMEM((2, 4, 4, 64, 128), BF),
+            pltpu.VMEM((2, 4, 3, 64, 128), BF),
             pltpu.VMEM((2, 16, 16, 128), BF),
             pltpu.VMEM((2, n_z, 16, 128), BF),
             pltpu.VMEM((2, 16, 128), BF),
@@ -431,20 +492,30 @@
             pltpu.VMEM((ROWS, D), BF),
             pltpu.VMEM((ROWS, D), BF),
             pltpu.VMEM((ROWS, D), F32),
+            dma((4,)),
             dma((4,)),
             pltpu.SemaphoreType.REGULAR((3,)),
             dma((2, N_G)), dma((2, N_G)),
             dma((2, N_G)), dma((2, N_G)),
             dma((2,)), dma((2,)),
             dma((5,)), dma((5,)),
-            dma((2, 2, 3)), dma((2, 2, 3)),
-            dma((2, 2, 3)), dma((2, 2, 3)),
+            dma((2, 4, 3)), dma((2, 4, 3)),
+            dma((2, 4, 3)), dma((2, 4, 3)),
             dma((2, n_z)), dma((2, n_z)),
             dma((2, NZ, 2)), dma((2,)),
         ],
-        compiler_params=pltpu.CompilerParams(collective_id=0, has_side_effects=True, vmem_limit_bytes=50 * 2**20),
+        compiler_params=pltpu.CompilerParams(collective_id=0, has_side_effects=True, vmem_limit_bytes=62 * 2**20),
         name="layer",
-    )(tokens, cotangent, valid, input_weight, output_weight)
+    )(tokens, cotangent, lengths, input_weight, output_weight)
+    return pl.pallas_call(
+        hand_over,
+        out_shape=shapes,
+        in_specs=[hbm] * 4,
+        out_specs=(hbm,) * 4,
+        scratch_shapes=[pltpu.VMEM(leaf.shape, leaf.dtype) for leaf in shapes] + [dma((2, 4))],
+        compiler_params=pltpu.CompilerParams(vmem_limit_bytes=62 * 2**20),
+        name="hand_over",
+    )(*made)
 
 
 def solution(mesh):

time: 81.5 us -> 78.3 us (0.961)
  local copies, waits for them, and re-layouts: 6.92 us -> 0 us
  Pallas kernels: 73 us -> 77.5 us
    unnamed x12 -> x0, local copies, waits for them, and re-layouts: 6.84 us -> none
    pallas_call x1 -> x2, Pallas kernels: 73 us -> 77.5 us  [the longest x1 75.2 us: per_device(): pl.pallas_call(kernel, out_shape=shapes, in_specs=[hbm, hbm, smem, hbm, h...]
where the time goes in v4:
time: 78.3 us; the launch traced here: 78.1 us
  Pallas kernels  77.5 us (99%)
    pallas_call x1, Pallas kernels, per_device(): pl.pallas_call(kernel, out_shape=shapes, in_specs=[hbm, hbm, smem, hbm, h...  75.2 us
    pallas_call x1, Pallas kernels, per_device(): pl.pallas_call(hand_over, out_shape=shapes, in_specs=[hbm] * 4, out_specs...  2.24 us

profile of v4, /device:TPU:1, one launch (start us, length us, event | category | flops | bytes accessed | tf_op | source)
XLA Modules:
  0.0 78.1 jit_solution(16968230211216401306)
XLA Ops:
  0.6 75.2 %layer.1 = (bf16[256,1024]{1,0:T(8,128)(2,1)}, bf16[256,1024]{1,0:T(8,128)(2,1)}, f32[64,1536]{1,0:T(8,128)}, f32[64,512]{1,0:T(8,128)}) custom-call(bf16[256,1024]{1,0:T(8,128)(2,1)} %tok_hbm.1, bf16[256,1024]{1,0:T(8,128)(2,1)} %cot_hbm.1, s32[8]{0:T(128)} %lengths_ref.1, bf16[64,1536]{1,0:T(8,128)(2,1)} %win_hbm.1, bf16[64,512]{1,0:T(8,128)(2,1)} %wout_hbm.1), custom_call_target="tpu_custom_call" | custom-call | tf_op jit(solution)/shard_map/layer/pallas_call | solution.py:453
  75.9 2.2 %hand_over.1 = (bf16[256,1024]{1,0:T(8,128)(2,1)}, bf16[256,1024]{1,0:T(8,128)(2,1)}, f32[64,1536]{1,0:T(8,128)}, f32[64,512]{1,0:T(8,128)}) custom-call(bf16[256,1024]{1,0:T(8,128)(2,1)} %get-tuple-element.8.refs_0_, bf16[256,1024]{1,0:T(8,128)(2,1)} %get-tuple-element.9.refs_1_, f32[64,1536]{1,0:T(8,128)} %get-tuple-element.10.refs_2_, ...), custom_call_target="tpu_custom_call" | custom-call | tf_op jit(solution)/shard_map/hand_over/pallas_call | solution.py:510

commit v5 on v4

--- a/solution.py
+++ b/solution.py
@@ -201,7 +201,7 @@
             real = (lens, lens2)[side][0:1, t * TILE : (t + 1) * TILE]
             allowed = causal & (key_place < jnp.concatenate([real, real], axis=1))
             raised.append(jnp.where(allowed, jnp.exp(sc * scale), 0.0))
-        prob = [e / jnp.sum(e, axis=0, keepdims=True) for e in raised]
+        prob = [e * (1.0 / jnp.sum(e, axis=0, keepdims=True)) for e in raised]
         for n, p in enumerate(prob):
             probs[n] = p
         rounded = [p.astype(BF) for p in prob]
@@ -267,52 +267,82 @@
             cp.start()
         return started
 
-    def second_end(i, started):
+    my_part = (z % 4) // 2
+
+    def line_copies(i, part):
+        base = z - z % 4 + 2 * part
+        far, near = [], []
+        for q in range(4):
+            for e in range(2):
+                to = (base + 4 * q + e) % NZ
+                k = 2 * q + e
+                cp = copy(acc.at[i, to], z_in.at[i, z], z_send.at[i, part, k], z_recv.at[i], device(x, y, to, c))
+                if q:
+                    far.append(cp)
+                else:
+                    near.append((to, cp))
+        return far, near
+
+    def second_end(i, part, started):
         for cp in started:
             cp.wait()
-        for g in range(4):
+        for g in (2 * part, 2 * part + 1):
             total = first_sum[i, g, x if g % 2 else y].astype(F32)
             for d in range(3):
                 total = total + second_in[i, g, d].astype(F32)
             total = total.astype(BF)
             for n in range(4):
                 acc[i, n * 4 + g] = total[n * 16 : (n + 1) * 16]
-        started = []
-        for dz in range(1, NZ):
-            tz = (z + dz) % NZ
-            started.append(copy(acc.at[i, tz], z_in.at[i, dz - 1], z_send.at[i, dz - 1], z_recv.at[i, dz - 1], device(x, y, tz, c)))
-        for cp in started:
+        far, near = line_copies(i, part)
+        for cp in far:
             cp.start()
-        return started
-
-    def line_end(i, started):
-        for cp in started:
-            cp.wait()
-        total = acc[i, z].astype(F32)
-        for j in range(NZ - 1):
-            total = total + z_in[i, j].astype(F32)
-        red[i] = total.astype(BF)
-        started = []
+        for to, cp in near:
+            @pl.when(to != z)
+            def _():
+                cp.start()
+
+        @pl.when(my_part == part)
+        def _():
+            pltpu.make_async_copy(acc.at[i, z], z_in.at[i, z], z_recv.at[i]).start()
+
+    def line_sent(i, part):
+        far, near = line_copies(i, part)
+        for cp in far:
+            cp.wait_send()
+        for to, cp in near:
+            @pl.when(to != z)
+            def _():
+                cp.wait_send()
+
+    def back_copies(i):
+        copies = []
         for dz in range(NZ):
             tz = (z + dz) % NZ
             for other in range(2):
                 if dz or other:
                     tx = xh * 2 + (xl + other) % 2
-                    started.append(copy(red.at[i], fin.at[i, c, z], f_send.at[i, dz, other], f_recv.at[i], device(tx, y, tz, xl)))
-        for cp in started:
-            cp.start()
-        beside = copy(red.at[i], fin.at[i, c, z], f_send.at[i, 0, 0], f_recv.at[i], sibling)
-        here = pltpu.make_async_copy(red.at[i], fin.at[i, c, z], f_recv.at[i])
-
-        @pl.when(c != xl)
+                    copies.append(copy(red.at[i], fin.at[i, c, z], f_send.at[i, dz, other], f_recv.at[i], device(tx, y, tz, xl)))
+        return copies, copy(red.at[i], fin.at[i, c, z], f_send.at[i, 0, 0], f_recv.at[i], sibling)
+
+    def line_end(i, part):
+        @pl.when(my_part == part)
         def _():
-            beside.start()
-
-        @pl.when(c == xl)
-        def _():
-            here.start()
-
-        return started, beside
+            pltpu.make_async_copy(z_in.at[i], z_in.at[i], z_recv.at[i]).wait()
+            total = z_in[i, 0].astype(F32)
+            for j in range(1, NZ):
+                total = total + z_in[i, j].astype(F32)
+            red[i] = total.astype(BF)
+            copies, beside = back_copies(i)
+            for cp in copies:
+                cp.start()
+
+            @pl.when(c != xl)
+            def _():
+                beside.start()
+
+            @pl.when(c == xl)
+            def _():
+                pltpu.make_async_copy(red.at[i], fin.at[i, c, z], f_recv.at[i]).start()
 
     def back_end(i):
         pltpu.make_async_copy(fin.at[i], fin.at[i], f_recv.at[i]).wait()
@@ -327,8 +357,9 @@
                 else:
                     gout_ref[rows, at : at + 128] = value
 
-    def back_sent(started, beside):
-        for cp in started:
+    def back_sent(i):
+        copies, beside = back_copies(i)
+        for cp in copies:
             cp.wait_send()
 
         @pl.when(c != xl)
@@ -359,6 +390,7 @@
     first1s = first_start(1, score_groups)
     second0s = first_end(0, score_groups, first0s)
     ready_wait(2)
+    second_end(0, 1, second0v)
 
     def head_sums(rows, cols):
         mixed = dot(att[0, rows, :], w[0, cols, 384:], 1, 1) + dot(att[1, rows, :], w[1, cols, 384:], 1, 1)
@@ -379,7 +411,9 @@
     for cp in backs:
         cp.start()
     second1v = first_end(1, values, first1v)
-    line0 = second_end(0, second0v + second0s)
+    second_end(0, 0, second0s)
+    second1s = first_end(1, score_groups, first1s)
+    second_end(1, 1, second1v)
 
     @pl.loop(0, 4)
     def _(t):
@@ -388,9 +422,10 @@
         lo_ref[:, cols] = (tok_ref[:, cols].astype(F32) + mixed).astype(BF)
         gn_own[:, cols] = back
 
-    second1s = first_end(1, score_groups, first1s)
-    line1 = second_end(1, second1v + second1s)
-    back0 = line_end(0, line0)
+    second_end(1, 0, second1s)
+    line_end(0, 1)
+    line_end(0, 0)
+    line_end(1, 1)
 
     for cp in backs:
         cp.wait()
@@ -413,13 +448,15 @@
     ]
     outs[0].start()
     outs[1].start()
-    back1 = line_end(1, line1)
+    line_end(1, 0)
     back_end(0)
     back_end(1)
     outs[2].start()
     outs[3].start()
-    back_sent(*back0)
-    back_sent(*back1)
+    for i in range(2):
+        line_sent(i, 0)
+        line_sent(i, 1)
+        back_sent(i)
     for cp in direct0 + direct1 + hands0 + hands1 + wides:
         cp.wait_send()
     for cp in outs:
@@ -443,7 +480,6 @@
 def per_device(tokens, lengths, cotangent, input_weight, output_weight):
     hbm, smem = pl.BlockSpec(memory_space=pl.ANY), pl.BlockSpec(memory_space=pltpu.SMEM)
     dma = pltpu.SemaphoreType.DMA
-    n_z = NZ - 1
     shapes = (
         jax.ShapeDtypeStruct((ROWS, D), BF),
         jax.ShapeDtypeStruct((ROWS, D), BF),
@@ -484,7 +520,7 @@
             pltpu.VMEM((2, 4, 4, 64, 128), BF),
             pltpu.VMEM((2, 4, 3, 64, 128), BF),
             pltpu.VMEM((2, 16, 16, 128), BF),
-            pltpu.VMEM((2, n_z, 16, 128), BF),
+            pltpu.VMEM((2, NZ, 16, 128), BF),
             pltpu.VMEM((2, 16, 128), BF),
             pltpu.VMEM((2, 2, 16, 16, 128), BF),
             pltpu.VMEM((ROWS, D), BF),
@@ -501,7 +537,7 @@
             dma((5,)), dma((5,)),
             dma((2, 4, 3)), dma((2, 4, 3)),
             dma((2, 4, 3)), dma((2, 4, 3)),
-            dma((2, n_z)), dma((2, n_z)),
+            dma((2, 2, 8)), dma((2,)),
             dma((2, NZ, 2)), dma((2,)),
         ],
         compiler_params=pltpu.CompilerParams(collective_id=0, has_side_effects=True, vmem_limit_bytes=62 * 2**20),

time: 78.3 us -> 76.2 us (0.973)
  Pallas kernels: 77.5 us -> 75.4 us
    pallas_call x1, Pallas kernels: 75.2 us -> 73.1 us  [per_device(): pl.pallas_call(kernel, out_shape=shapes, in_specs=[hbm, hbm, smem, hbm, h...]
where the time goes in v5:
time: 76.2 us; the launch traced here: 76 us
  Pallas kernels  75.4 us (99%)
    pallas_call x1, Pallas kernels, per_device(): pl.pallas_call(kernel, out_shape=shapes, in_specs=[hbm, hbm, smem, hbm, h...  73.1 us
    pallas_call x1, Pallas kernels, per_device(): pl.pallas_call(hand_over, out_shape=shapes, in_specs=[hbm] * 4, out_specs...  2.24 us

profile of v5, /device:TPU:1, one launch (start us, length us, event | category | flops | bytes accessed | tf_op | source)
XLA Modules:
  0.0 76.0 jit_solution(16049770045859410133)
XLA Ops:
  0.6 73.1 %layer.1 = (bf16[256,1024]{1,0:T(8,128)(2,1)}, bf16[256,1024]{1,0:T(8,128)(2,1)}, f32[64,1536]{1,0:T(8,128)}, f32[64,512]{1,0:T(8,128)}) custom-call(bf16[256,1024]{1,0:T(8,128)(2,1)} %tok_hbm.1, bf16[256,1024]{1,0:T(8,128)(2,1)} %cot_hbm.1, s32[8]{0:T(128)} %lengths_ref.1, bf16[64,1536]{1,0:T(8,128)(2,1)} %win_hbm.1, bf16[64,512]{1,0:T(8,128)(2,1)} %wout_hbm.1), custom_call_target="tpu_custom_call" | custom-call | tf_op jit(solution)/shard_map/layer/pallas_call | solution.py:489
  73.8 2.2 %hand_over.1 = (bf16[256,1024]{1,0:T(8,128)(2,1)}, bf16[256,1024]{1,0:T(8,128)(2,1)}, f32[64,1536]{1,0:T(8,128)}, f32[64,512]{1,0:T(8,128)}) custom-call(bf16[256,1024]{1,0:T(8,128)(2,1)} %get-tuple-element.8.refs_0_, bf16[256,1024]{1,0:T(8,128)(2,1)} %get-tuple-element.9.refs_1_, f32[64,1536]{1,0:T(8,128)} %get-tuple-element.10.refs_2_, ...), custom_call_target="tpu_custom_call" | custom-call | tf_op jit(solution)/shard_map/hand_over/pallas_call | solution.py:546

commit v6 on v5

--- a/solution.py
+++ b/solution.py
@@ -158,12 +158,12 @@
         direct0[j].wait_recv()
         hands0.append(hand_start(0, j))
     direct1 = direct_start(1)
+    for cp in shares:
+        cp.wait()
+    normalise(tok2, cot2, ROWS)
     for j in range(6, N_G):
         direct0[j].wait_recv()
         hands0.append(hand_start(0, j))
-    for cp in shares:
-        cp.wait()
-    normalise(tok2, cot2, ROWS)
     ready_wait(1)
     ready_signal(2)
 
@@ -370,10 +370,13 @@
     gather_end(0, hands0)
     project(0)
     hands1 = []
-    for j in range(N_G):
+    for j in range(8):
         direct1[j].wait_recv()
         hands1.append(hand_start(1, j))
     attend(0)
+    for j in range(8, N_G):
+        direct1[j].wait_recv()
+        hands1.append(hand_start(1, j))
     products_values(0)
     first0v = first_start(0, values)
     attend_back(0)
@@ -411,8 +414,8 @@
     for cp in backs:
         cp.start()
     second1v = first_end(1, values, first1v)
+    second1s = first_end(1, score_groups, first1s)
     second_end(0, 0, second0s)
-    second1s = first_end(1, score_groups, first1s)
     second_end(1, 1, second1v)
 
     @pl.loop(0, 4)
@@ -443,16 +446,18 @@
     outs = [
         pltpu.make_async_copy(lo_ref, lo_hbm, o_sem.at[0]),
         pltpu.make_async_copy(gt_ref, gt_hbm, o_sem.at[1]),
-        pltpu.make_async_copy(gin_ref, gin_hbm, o_sem.at[2]),
-        pltpu.make_async_copy(gout_ref, gout_hbm, o_sem.at[3]),
+        pltpu.make_async_copy(gout_ref, gout_hbm, o_sem.at[2]),
     ]
+    for n in range(4):
+        rows = pl.ds(n * 16, 16)
+        outs.append(pltpu.make_async_copy(gin_ref.at[rows], gin_hbm.at[rows], o_sem.at[3 + n]))
     outs[0].start()
     outs[1].start()
     line_end(1, 0)
     back_end(0)
     back_end(1)
-    outs[2].start()
-    outs[3].start()
+    for cp in outs[2:]:
+        cp.start()
     for i in range(2):
         line_sent(i, 0)
         line_sent(i, 1)
@@ -464,10 +469,14 @@
 
 
 def hand_over(*refs):
-    sems = refs[-1]
-    here = refs[8:12]
-    loads = [pltpu.make_async_copy(src, mid, sems.at[0, j]) for j, (src, mid) in enumerate(zip(refs[:4], here))]
-    stores = [pltpu.make_async_copy(mid, dst, sems.at[1, j]) for j, (mid, dst) in enumerate(zip(here, refs[4:8]))]
+    sems, here = refs[-1], refs[8:12]
+    loads, stores = [], []
+    for j, (src, mid, dst) in enumerate(zip(refs[:4], here, refs[4:8])):
+        size = src.shape[0] // 4
+        for n in range(4):
+            rows = pl.ds(n * size, size)
+            loads.append(pltpu.make_async_copy(src.at[rows], mid.at[rows], sems.at[0, j, n]))
+            stores.append(pltpu.make_async_copy(mid.at[rows], dst.at[rows], sems.at[1, j, n]))
     for cp in loads:
         cp.start()
     for load, store in zip(loads, stores):
@@ -529,7 +538,7 @@
             pltpu.VMEM((ROWS, D), BF),
             pltpu.VMEM((ROWS, D), F32),
             dma((4,)),
-            dma((4,)),
+            dma((7,)),
             pltpu.SemaphoreType.REGULAR((3,)),
             dma((2, N_G)), dma((2, N_G)),
             dma((2, N_G)), dma((2, N_G)),
@@ -548,7 +557,7 @@
         out_shape=shapes,
         in_specs=[hbm] * 4,
         out_specs=(hbm,) * 4,
-        scratch_shapes=[pltpu.VMEM(leaf.shape, leaf.dtype) for leaf in shapes] + [dma((2, 4))],
+        scratch_shapes=[pltpu.VMEM(leaf.shape, leaf.dtype) for leaf in shapes] + [dma((2, 4, 4))],
         compiler_params=pltpu.CompilerParams(vmem_limit_bytes=62 * 2**20),
         name="hand_over",
     )(*made)

time: 76.2 us -> 76.4 us (level)
  no operation moved by 1% of the time
where the time goes in v6:
time: 76.4 us; the launch traced here: 76.2 us
  Pallas kernels  75.6 us (99%)
    pallas_call x1, Pallas kernels, per_device(): pl.pallas_call(kernel, out_shape=shapes, in_specs=[hbm, hbm, smem, hbm, h...  73.2 us
    pallas_call x1, Pallas kernels, per_device(): pl.pallas_call(hand_over, out_shape=shapes, in_specs=[hbm] * 4, out_specs...  2.39 us

profile of v6, /device:TPU:1, one launch (start us, length us, event | category | flops | bytes accessed | tf_op | source)
XLA Modules:
  0.0 76.2 jit_solution(17923857484982872121)
XLA Ops:
  0.6 73.2 %layer.1 = (bf16[256,1024]{1,0:T(8,128)(2,1)}, bf16[256,1024]{1,0:T(8,128)(2,1)}, f32[64,1536]{1,0:T(8,128)}, f32[64,512]{1,0:T(8,128)}) custom-call(bf16[256,1024]{1,0:T(8,128)(2,1)} %tok_hbm.1, bf16[256,1024]{1,0:T(8,128)(2,1)} %cot_hbm.1, s32[8]{0:T(128)} %lengths_ref.1, bf16[64,1536]{1,0:T(8,128)(2,1)} %win_hbm.1, bf16[64,512]{1,0:T(8,128)(2,1)} %wout_hbm.1), custom_call_target="tpu_custom_call" | custom-call | tf_op jit(solution)/shard_map/layer/pallas_call | solution.py:498
  73.8 2.4 %hand_over.1 = (bf16[256,1024]{1,0:T(8,128)(2,1)}, bf16[256,1024]{1,0:T(8,128)(2,1)}, f32[64,1536]{1,0:T(8,128)}, f32[64,512]{1,0:T(8,128)}) custom-call(bf16[256,1024]{1,0:T(8,128)(2,1)} %get-tuple-element.8.refs_0_, bf16[256,1024]{1,0:T(8,128)(2,1)} %get-tuple-element.9.refs_1_, f32[64,1536]{1,0:T(8,128)} %get-tuple-element.10.refs_2_, ...), custom_call_target="tpu_custom_call" | custom-call | tf_op jit(solution)/shard_map/hand_over/pallas_call | solution.py:555

commit v7 on v6

--- a/solution.py
+++ b/solution.py
@@ -189,9 +189,9 @@
         return jnp.where(first_head, both[:TILE], both[TILE:])
 
     def project(i):
+        proj[...] = dot(normed[...], w[i, :, :384], 1, 0).astype(BF)
         for r, src in enumerate((cot_ref, cot2)):
             own = slice(r * 256, (r + 1) * 256)
-            proj[own, :] = dot(normed[own, :], w[i, :, :384], 1, 0).astype(BF)
             gatt[own, :] = dot(src[...], w[i, :, 384:], 1, 0).astype(BF)
 
     def attend(i):
@@ -222,23 +222,21 @@
             grads[i, r, :128] = unstack(dot(gs, proj[r, 128:256], 0, 0)).astype(BF)
 
     def products_values(i):
-        @pl.loop(0, 4)
-        def _(t):
-            rows = pl.ds(pl.multiple_of(t * 256, 256), 256)
-            terms[i, 2, t] = dot(normed_t[rows, :], grads[i, :, 256:], 1, 0).astype(BF).reshape(4, 64, 128)
-            terms[i, 3, t] = dot(cot_t[rows, :], att[i], 1, 0).astype(BF).reshape(4, 64, 128)
+        for t in range(2):
+            rows = slice(t * 512, (t + 1) * 512)
+            terms[i, 2, 2 * t : 2 * t + 2] = dot(normed_t[rows, :], grads[i, :, 256:], 1, 0).astype(BF).reshape(2, 4, 64, 128)
+            terms[i, 3, 2 * t : 2 * t + 2] = dot(cot_t[rows, :], att[i], 1, 0).astype(BF).reshape(2, 4, 64, 128)
 
     def products_scores(i):
-        @pl.loop(0, 4)
-        def _(t):
-            rows = pl.ds(pl.multiple_of(t * 256, 256), 256)
+        for t in range(2):
+            rows = slice(t * 512, (t + 1) * 512)
             both = dot(normed_t[rows, :], grads[i, :, :256], 1, 0).astype(BF)
-            terms[i, 0, t] = both[:, :128].reshape(4, 64, 128)
-            terms[i, 1, t] = both[:, 128:].reshape(4, 64, 128)
+            terms[i, 0, 2 * t : 2 * t + 2] = both[:, :128].reshape(2, 4, 64, 128)
+            terms[i, 1, 2 * t : 2 * t + 2] = both[:, 128:].reshape(2, 4, 64, 128)
 
     def first_start(i, groups):
         started = []
-        for d in (1, 2, 3):
+        for d in (2, 1, 3):
             tx, ty = (x + d) % NX, (y + d) % NY
             for g in groups:
                 src = terms.at[i, g, ty] if g % 2 else terms.at[i, g, :, tx]
@@ -258,7 +256,7 @@
                     total = total + first_in[i, g, d, n].astype(F32)
                 first_sum[i, g, n] = total.astype(BF)
         started = []
-        for d in (1, 2, 3):
+        for d in (2, 1, 3):
             tx, ty = (x + d) % NX, (y + d) % NY
             for g in groups:
                 to = device(tx, y, z, c) if g % 2 else device(x, ty, z, c)
@@ -272,7 +270,7 @@
     def line_copies(i, part):
         base = z - z % 4 + 2 * part
         far, near = [], []
-        for q in range(4):
+        for q in (2, 1, 3, 0):
             for e in range(2):
                 to = (base + 4 * q + e) % NZ
                 k = 2 * q + e
@@ -316,7 +314,7 @@
 
     def back_copies(i):
         copies = []
-        for dz in range(NZ):
+        for dz in sorted(range(NZ), key=lambda d: -min(d, NZ - d)):
             tz = (z + dz) % NZ
             for other in range(2):
                 if dz or other:

time: 76.4 us -> 74.2 us (0.971)
  Pallas kernels: 75.6 us -> 73.4 us
    pallas_call x1, Pallas kernels: 73.2 us -> 71 us  [per_device(): pl.pallas_call(kernel, out_shape=shapes, in_specs=[hbm, hbm, smem, hbm, h...]
where the time goes in v7:
time: 74.2 us; the launch traced here: 74 us
  Pallas kernels  73.4 us (99%)
    pallas_call x1, Pallas kernels, per_device(): pl.pallas_call(kernel, out_shape=shapes, in_specs=[hbm, hbm, smem, hbm, h...  71 us
    pallas_call x1, Pallas kernels, per_device(): pl.pallas_call(hand_over, out_shape=shapes, in_specs=[hbm] * 4, out_specs...  2.39 us

profile of v7, /device:TPU:1, one launch (start us, length us, event | category | flops | bytes accessed | tf_op | source)
XLA Modules:
  0.0 74.0 jit_solution(2047305398380394407)
XLA Ops:
  0.6 71.0 %layer.1 = (bf16[256,1024]{1,0:T(8,128)(2,1)}, bf16[256,1024]{1,0:T(8,128)(2,1)}, f32[64,1536]{1,0:T(8,128)}, f32[64,512]{1,0:T(8,128)}) custom-call(bf16[256,1024]{1,0:T(8,128)(2,1)} %tok_hbm.1, bf16[256,1024]{1,0:T(8,128)(2,1)} %cot_hbm.1, s32[8]{0:T(128)} %lengths_ref.1, bf16[64,1536]{1,0:T(8,128)(2,1)} %win_hbm.1, bf16[64,512]{1,0:T(8,128)(2,1)} %wout_hbm.1), custom_call_target="tpu_custom_call" | custom-call | tf_op jit(solution)/shard_map/layer/pallas_call | solution.py:496
  71.6 2.4 %hand_over.1 = (bf16[256,1024]{1,0:T(8,128)(2,1)}, bf16[256,1024]{1,0:T(8,128)(2,1)}, f32[64,1536]{1,0:T(8,128)}, f32[64,512]{1,0:T(8,128)}) custom-call(bf16[256,1024]{1,0:T(8,128)(2,1)} %get-tuple-element.8.refs_0_, bf16[256,1024]{1,0:T(8,128)(2,1)} %get-tuple-element.9.refs_1_, f32[64,1536]{1,0:T(8,128)} %get-tuple-element.10.refs_2_, ...), custom_call_target="tpu_custom_call" | custom-call | tf_op jit(solution)/shard_map/hand_over/pallas_call | solution.py:553
